TPU v7x, 32 devices: a whole 2x2x4 slice. The times are simulated.
32 devices in a mesh: vox: 8 (over z, core), fsdp: 4 (over y, x).
Axes of the slice: x: 2, y: 2, z: 4, core: 2. Of those that a mesh axis runs over, the one named last changes fastest.
Arguments:
- tokens: bfloat16 [4, 3072, 1024], P('fsdp', 'vox'), may hold values from -6 to 6
- gain: float32 [1024], replicated, may hold values from 0.5 to 1.5
- w_qkv: bfloat16 [1024, 3072], P('fsdp'), may hold values from -0.1875 to 0.1875
- w_out: bfloat16 [1024, 1024], P('fsdp'), may hold values from -0.1875 to 0.1875
- logit_scale: float32 [16], replicated, may hold values from 4 to 240
- key_blocks: int32 [4, 48, 8], P('fsdp', 'vox'), may hold values from 0 to 47, as said below
- slot_count: int32 [4, 48], P('fsdp', 'vox'), may hold values from 1 to 8, as said below
- valid_voxels: int32 [4, 48], P('fsdp'), may hold values from 8 to 64
- cotangent: bfloat16 [4, 3072, 1024], P('fsdp', 'vox'), may hold values from -6 to 6
Outputs:
- mixed: bfloat16 [4, 3072, 1024], P('fsdp', 'vox')
- d_tokens: bfloat16 [4, 3072, 1024], P('fsdp', 'vox')
- d_wqkv: float32 [1024, 3072], P('fsdp', 'vox')
- d_wout: float32 [1024, 1024], P('fsdp', 'vox')
- d_gain: float32 [1024], replicated
- d_scale: float32 [16], replicated
Inputs may be any that keep to these rules, and one draw needn't show every extreme that they name: `key_blocks`: slot 0 of every block names the block itself; every listed block lies in the same scene within 3 blocks of its query block, and that distance is reached. Slots from slot_count on are not used.
All inputs are finite; a program needn't handle non-finite values.
Results may differ from a plain program's by a relative error of at most 0.012.
The roundings to bfloat16 on the way count: a program that leaves them out, or rounds other values in their place, can miss the bound.
Values may be sent and summed in bfloat16 or wider, within the bound.
No kernel may reach another device: no remote copies, remote signals or barrier semaphores. Data moves between devices by JAX's collectives and lax.ppermute only.
A program may use at most 128 MiB of HBM per device.

v0:
```python
import functools

import jax
import jax.numpy as jnp
from jax import lax
from jax.experimental import pallas as pl
from jax.experimental.pallas import tpu as pltpu
from jax.sharding import PartitionSpec as P

HEADS = 16
HD = 64
PAIR = 2 * HD
BLK = 64
WINDOW = 8
EPS = 1e-06
LOG2E = 1.4426950408889634
BF = jnp.bfloat16
F32 = jnp.float32


def dot(a, b, dims=((1,), (0,))):
    return lax.dot_general(a, b, (dims, ((), ())), preferred_element_type=F32)


def head_sums(x, same_head):
    high = x.astype(BF)
    low = (x - high.astype(F32)).astype(BF)
    return dot(high, same_head) + dot(low, same_head)


def unit_rows(x, same_head):
    length = jnp.sqrt(head_sums(x * x, same_head) + EPS)
    return x / length, length


def unit_back(unit, length, grad, same_head):
    return (grad - unit * head_sums(unit * grad, same_head)) / length


def attention_kernel(
    mult_ref, valid_ref, scale_ref, even_ref,
    q_ref, k_ref, v_ref, k1_ref, v1_ref, k2_ref, v2_ref, u_ref,
    *refs,
):
    carried, refs = (refs[:3], refs[3:]) if len(refs) > 22 else ((), refs)
    att_ref, dq_ref, dk_ref, dv_ref, rim1_ref, rim2_ref, ds_ref, turn_ref = refs[:8]
    k_unit, k_len, k_low, k_turn, v_low, v_turn, bias = refs[8:15]
    scores, grads, raised, w_lows, c_lows, dk, dv = refs[15:]
    held = slice(PAIR, 2 * PAIR) if carried else slice(0, PAIR)
    if carried:
        att_ref[:, :PAIR] = carried[0][...]
        rim1_ref[:, :, :PAIR] = carried[1][...]
        rim2_ref[:, :, :PAIR] = carried[2][...]
    rows = q_ref.shape[0]
    margin = k1_ref.shape[0]
    even = even_ref[0] == 1
    pool = rows + 2 * margin
    reach = margin // BLK
    steps = rows // PAIR
    span = WINDOW * BLK
    pair = pl.program_id(0)

    lane = lax.broadcasted_iota(jnp.int32, (BLK, PAIR), 1)
    row = lax.broadcasted_iota(jnp.int32, (BLK, PAIR), 0)
    head_a = lax.broadcasted_iota(jnp.int32, (PAIR, PAIR), 0) < HD
    head_b = lax.broadcasted_iota(jnp.int32, (PAIR, PAIR), 1) < HD
    same_head = jnp.where(head_a == head_b, 1.0, 0.0).astype(BF)
    first_lanes = head_b

    @pl.when(pair == 0)
    def _():
        for t in range(steps):
            for w in range(WINDOW):
                count = jnp.where(lane < BLK, mult_ref[2 * t, w], mult_ref[2 * t + 1, w])
                live = row < valid_ref[2 * t + w]
                seen = jnp.where(live, count, 0).astype(F32)
                bias[t, w * BLK : (w + 1) * BLK, :] = jnp.where(
                    seen > 0.0, jnp.log2(jnp.maximum(seen, 1.0)), -1e30
                )

    def split_heads(x):
        return jnp.concatenate(
            [jnp.where(first_lanes, x, 0.0), jnp.where(first_lanes, 0.0, x)], axis=0
        ).astype(BF)

    def take(at, keys, values):
        unit, length = unit_rows(keys.astype(F32), same_head)
        place = slice(at, at + keys.shape[0])
        k_unit[place, :] = unit
        k_len[place, :] = length
        k_low[place, :] = unit.astype(BF)
        v_low[place, :] = values

    for part in range(0, margin, BLK):
        here = slice(part, part + BLK)
        k1, k2 = k1_ref[here, :].astype(F32), k2_ref[here, :].astype(F32)
        v1, v2 = v1_ref[here, :].astype(F32), v2_ref[here, :].astype(F32)
        take(part, jnp.where(even, k2, k1), jnp.where(even, v2, v1).astype(BF))
        take(margin + rows + part, jnp.where(even, k1, k2), jnp.where(even, v1, v2).astype(BF))
    for part in range(0, rows, PAIR):
        here = slice(part, part + PAIR)
        take(margin + part, k_ref[here, :], v_ref[here, :])
    for part in range(0, pool, 128):
        place = slice(part, part + 128)
        k_turn[:, place] = jnp.transpose(k_low[place, :].astype(F32)).astype(BF)
        v_turn[:, place] = jnp.transpose(v_low[place, :].astype(F32)).astype(BF)

    dk[...] = jnp.zeros_like(dk)
    dv[...] = jnp.zeros_like(dv)
    wide_lane = lax.broadcasted_iota(jnp.int32, (1, 2 * PAIR), 1)
    scale = jnp.where(wide_lane < PAIR, scale_ref[2 * pair], scale_ref[2 * pair + 1])
    ds = jnp.zeros((8, 2 * PAIR), F32)

    def window_of(t):
        return slice(t * PAIR, t * PAIR + span)

    def begin(t):
        own, window = slice(t * PAIR, (t + 1) * PAIR), window_of(t)
        q_unit, q_len = unit_rows(q_ref[own, :].astype(F32), same_head)
        q_split = split_heads(q_unit)
        live = jnp.concatenate(
            [row < valid_ref[2 * t + reach], row < valid_ref[2 * t + 1 + reach]], axis=0
        )
        u_split = split_heads(jnp.where(live, u_ref[own, :].astype(F32), 0.0))
        scores[t % 2] = dot(k_low[window, :], q_split, ((1,), (1,)))
        grads[t % 2] = dot(v_low[window, :], u_split, ((1,), (1,)))
        return q_unit, q_len, q_split, live, u_split

    stretch = scale * LOG2E
    parts = [slice(i, i + 32) for i in range(0, span, 32)]

    def fold(x):
        return x.reshape(4, 8, 2 * PAIR)

    following = begin(0)
    for t in range(steps):
        own, window = slice(t * PAIR, (t + 1) * PAIR), window_of(t)
        q_unit, q_len, q_split, live, u_split = following
        s_ref, g_ref, e_ref = scores.at[t % 2], grads.at[t % 2], raised.at[t % 2]
        w_low, c_low = w_lows.at[t % 2], c_lows.at[t % 2]
        if t + 1 < steps:
            following = begin(t + 1)

        peak = jnp.full((8, 2 * PAIR), -1e30, F32)
        for part in parts:
            half = bias[t, part, :]
            x = s_ref[part, :] * stretch + jnp.concatenate([half, half], axis=1)
            e_ref[part, :] = x
            peak = jnp.maximum(peak, jnp.max(fold(x), axis=0))
        peak = jnp.max(peak, axis=0, keepdims=True)
        total = jnp.zeros((8, 2 * PAIR), F32)
        centre = jnp.zeros((8, 2 * PAIR), F32)
        for part in parts:
            e = jnp.exp2(e_ref[part, :] - peak)
            e_ref[part, :] = e
            total = total + jnp.sum(fold(e), axis=0)
            centre = centre + jnp.sum(fold(e * g_ref[part, :]), axis=0)
        share = 1.0 / jnp.sum(total, axis=0, keepdims=True)
        centre = jnp.sum(centre, axis=0, keepdims=True) * share
        for part in parts:
            w = e_ref[part, :] * share
            w_low[part, :] = w.astype(BF)
            sg = w * (g_ref[part, :] - centre)
            ds = ds + jnp.sum(fold(sg * s_ref[part, :]), axis=0)
            c_low[part, :] = (sg * scale).astype(BF)

        def own_heads(turned):
            return jnp.concatenate([turned[:HD, :PAIR], turned[HD:, PAIR:]], axis=0)

        mixed = own_heads(dot(v_turn[:, window], w_low[...]))
        att_ref[own, held] = jnp.where(live, jnp.transpose(mixed), 0.0).astype(BF)
        row_lane = lax.broadcasted_iota(jnp.int32, (PAIR, PAIR), 1)
        limit = jnp.where(
            row_lane < BLK, valid_ref[2 * t + reach], valid_ref[2 * t + 1 + reach] + BLK
        )
        turn_ref[:, own] = jnp.where(row_lane < limit, mixed, 0.0).astype(BF)
        q_grad = jnp.transpose(own_heads(dot(k_turn[:, window], c_low[...])))
        dq_ref[own, :] = unit_back(q_unit, q_len, q_grad, same_head).astype(BF)
        dv[window, :] += dot(w_low[...], u_split)
        dk[window, :] += dot(c_low[...], q_split)

    def key_grad(part):
        place = slice(part, part + BLK)
        return unit_back(k_unit[place, :], k_len[place, :], dk[place, :], same_head)

    for part in range(0, rows, BLK):
        here = slice(part, part + BLK)
        dk_ref[here, :] = key_grad(margin + part)
        dv_ref[here, :] = dv[margin + part : margin + part + BLK, :]
    for part in range(0, margin, BLK):
        here = slice(part, part + BLK)
        far = margin + rows + part
        kb, ka = key_grad(part), key_grad(far)
        vb, va = dv[part : part + BLK, :], dv[far : far + BLK, :]
        rim1_ref[0, here, held] = jnp.where(even, ka, kb).astype(BF)
        rim1_ref[1, here, held] = jnp.where(even, va, vb).astype(BF)
        rim2_ref[0, here, held] = jnp.where(even, kb, ka).astype(BF)
        rim2_ref[1, here, held] = jnp.where(even, vb, va).astype(BF)
    ds_ref[0, :, :] = ds


def attention(packed, first, second, upstream, mult, valid, scales, even, pairs, begin=0, count=2, base=0, carried=()):
    rows = packed.shape[0]
    width = count * PAIR
    both = width + (PAIR if carried else 0)
    margin = first.shape[0]
    pool = rows + 2 * margin
    held = len(pairs)
    stride = pairs[1] - pairs[0]
    steps = rows // PAIR
    span = WINDOW * BLK

    def at(offset):
        return lambda p, *_: (0, offset + p)

    return pl.pallas_call(
        attention_kernel,
        grid_spec=pltpu.PrefetchScalarGridSpec(
            num_scalar_prefetch=4,
            grid=(count,),
            in_specs=[
                pl.BlockSpec((rows, PAIR), at(begin)),
                pl.BlockSpec((rows, PAIR), at(held + begin)),
                pl.BlockSpec((rows, PAIR), at(2 * held + begin)),
                pl.BlockSpec((margin, PAIR), at(base + begin)),
                pl.BlockSpec((margin, PAIR), at(base + held + begin)),
                pl.BlockSpec((margin, PAIR), at(base + begin)),
                pl.BlockSpec((margin, PAIR), at(base + held + begin)),
                pl.BlockSpec((rows, PAIR), lambda p, *_: (0, pairs[begin] + stride * p)),
            ]
            + [whole(array.shape) for array in carried],
            out_specs=[
                pl.BlockSpec((rows, both // count), at(0)),
                pl.BlockSpec((rows, PAIR), at(0)),
                pl.BlockSpec((rows, PAIR), at(0)),
                pl.BlockSpec((rows, PAIR), at(0)),
                pl.BlockSpec((2, margin, both // count), lambda p, *_: (0, 0, p)),
                pl.BlockSpec((2, margin, both // count), lambda p, *_: (0, 0, p)),
                pl.BlockSpec((1, 8, 2 * PAIR), lambda p, *_: (p, 0, 0)),
                pl.BlockSpec((PAIR, rows), lambda p, *_: (p, 0)),
            ],
            scratch_shapes=[
                pltpu.VMEM((pool, PAIR), F32),
                pltpu.VMEM((pool, PAIR), F32),
                pltpu.VMEM((pool, PAIR), BF),
                pltpu.VMEM((PAIR, pool), BF),
                pltpu.VMEM((pool, PAIR), BF),
                pltpu.VMEM((PAIR, pool), BF),
                pltpu.VMEM((steps, span, PAIR), F32),
                pltpu.VMEM((2, span, 2 * PAIR), F32),
                pltpu.VMEM((2, span, 2 * PAIR), F32),
                pltpu.VMEM((2, span, 2 * PAIR), F32),
                pltpu.VMEM((2, span, 2 * PAIR), BF),
                pltpu.VMEM((2, span, 2 * PAIR), BF),
                pltpu.VMEM((pool, PAIR), F32),
                pltpu.VMEM((pool, PAIR), F32),
            ],
        ),
        out_shape=[
            jax.ShapeDtypeStruct((rows, both), BF),
            jax.ShapeDtypeStruct((rows, width), BF),
            jax.ShapeDtypeStruct((rows, width), F32),
            jax.ShapeDtypeStruct((rows, width), F32),
            jax.ShapeDtypeStruct((2, margin, both), BF),
            jax.ShapeDtypeStruct((2, margin, both), BF),
            jax.ShapeDtypeStruct((count, 8, 2 * PAIR), F32),
            jax.ShapeDtypeStruct((width, rows), BF),
        ],
        compiler_params=pltpu.CompilerParams(vmem_limit_bytes=24 * 1024 * 1024),
        cost_estimate=pl.CostEstimate(
            flops=8 * 2 * 6 * count * steps * span * 256 * 128,
            bytes_accessed=rows * width * 20,
            transcendentals=count * steps * span * 256,
        ),
        name="block_attention",
    )(
        mult, valid, scales, even,
        packed, packed, packed, first, first, second, second, upstream, *carried,
    )


def pick_kernel(core_ref, qkv_ref, out_ref, top_ref, low_ref):
    core = core_ref[0]
    at = 0
    for pairs in CHUNKS:
        for base in range(0, qkv_ref.shape[1], 8 * PAIR):
            for p in pairs:
                start = pl.multiple_of(base + 2 * p * PAIR + core * PAIR, PAIR)
                top_ref[:, at : at + PAIR] = qkv_ref[:PAIR, pl.ds(start, PAIR)]
                low_ref[:, at : at + PAIR] = qkv_ref[PAIR:, pl.ds(start, PAIR)]
                at += PAIR
    half = out_ref.shape[1] // 2
    rows = out_ref[pl.ds(pl.multiple_of(core * PAIR, PAIR), PAIR), :]
    top_ref[:, at:] = rows[:, :half]
    low_ref[:, at:] = rows[:, half:]


def whole(shape):
    return pl.BlockSpec(shape, lambda *_: (0,) * len(shape))


def small_kernel(kernel, name, scalars, arrays, outs, scratch=()):
    return pl.pallas_call(
        kernel,
        grid_spec=pltpu.PrefetchScalarGridSpec(
            num_scalar_prefetch=len(scalars),
            grid=(1,),
            in_specs=[whole(a.shape) for a in arrays],
            out_specs=[whole(shape) for shape, _ in outs],
            scratch_shapes=list(scratch),
        ),
        out_shape=[jax.ShapeDtypeStruct(shape, kind) for shape, kind in outs],
        compiler_params=pltpu.CompilerParams(vmem_limit_bytes=24 * 1024 * 1024),
        name=name,
    )(*scalars, *arrays)


def pick_weights(w_qkv, w_out, core_flag):
    height, columns = w_qkv.shape
    wide = columns // 2 + w_out.shape[1] // 2
    return small_kernel(
        pick_kernel, "pick_weights", [core_flag], [w_qkv, w_out], [((height // 2, wide), BF)] * 2
    )


def turn_kernel(x_ref, turned_ref):
    for i in range(0, x_ref.shape[0], PAIR):
        for j in range(0, x_ref.shape[1], PAIR):
            tile = x_ref[i : i + PAIR, j : j + PAIR].astype(F32)
            turned_ref[j : j + PAIR, i : i + PAIR] = jnp.transpose(tile).astype(BF)


def rim_kernel(even_ref, *refs):
    t_ref, rim1_ref, rim2_ref = refs[:3]
    even = even_ref[0] == 1
    margin = rim1_ref.shape[1]
    size = t_ref.shape[0] // 4

    def added(index, grad):
        rows = grad.shape[0]
        one, two = rim1_ref[index].astype(F32), rim2_ref[index].astype(F32)
        return jnp.concatenate(
            [
                grad[:margin] + jnp.where(even, two, one),
                grad[margin : rows - margin],
                grad[rows - margin :] + jnp.where(even, one, two),
            ],
            axis=0,
        ).astype(BF)

    if len(refs) == 10:
        q_ref, dk_ref, dv_ref, left_ref, right_ref, x_ref, y_ref = refs[3:]
        keys, values = added(0, dk_ref[...]), added(1, dv_ref[...])
        left_ref[:, : 2 * PAIR] = q_ref[...]
        left_ref[:, 2 * PAIR :] = keys[:, :PAIR]
        right_ref[:, :PAIR] = keys[:, PAIR:]
        right_ref[:, PAIR:] = values
    else:
        ka_ref, kb_ref, va_ref, vb_ref, left_ref, right_ref, x_ref, y_ref = refs[3:]
        left_ref[...] = added(0, jnp.concatenate([ka_ref[...], kb_ref[...]], axis=1))
        right_ref[...] = added(1, jnp.concatenate([va_ref[...], vb_ref[...]], axis=1))
    x_ref[...] = dot(t_ref[: 2 * size, :], left_ref[...]).astype(BF)
    y_ref[...] = dot(t_ref[size : 3 * size, :], right_ref[...]).astype(BF)


def leave_kernel(
    scene_ref, t_ref, a0_ref, a1_ref, a2_ref, cot_ref, q1_ref, q2_ref, left_ref, right_ref, fx_ref, fy_ref,
    x_ref, y_ref, kl_ref, kr_ref, e_ref, o_ref, at_ref,
):
    size = t_ref.shape[0] // 4
    quarter = cot_ref.shape[1] // 4
    at_ref[0] = a0_ref[:PAIR, :]
    at_ref[3] = a0_ref[PAIR:, :]
    at_ref[1] = a1_ref[...]
    at_ref[2] = a2_ref[...]
    x_ref[: 2 * size, :PAIR] = dot(t_ref[: 2 * size, :], q1_ref[...]).astype(BF)
    y_ref[: 2 * size, :PAIR] = dot(t_ref[size : 3 * size, :], q2_ref[...]).astype(BF)
    for i, k in enumerate(ORDER):
        grad = dot(at_ref[jnp.bitwise_xor(scene_ref[0], k)], cot_ref[...])
        evens = jnp.concatenate(
            [grad[:, :quarter], grad[:, 2 * quarter : 3 * quarter]], axis=0
        )
        odds = jnp.concatenate(
            [grad[:, quarter : 2 * quarter], grad[:, 3 * quarter :]], axis=0
        )
        if i < 2:
            x_ref[i * size : (i + 1) * size, PAIR:] = evens.astype(BF)
        else:
            e_ref[i - 2] = evens
        if i in (1, 2):
            y_ref[(i - 1) * size : i * size, PAIR:] = odds.astype(BF)
        else:
            o_ref[i // 3] = odds
    left, right = left_ref[...], right_ref[...]
    y_ref[2 * size :, :] = (
        dot(t_ref[2 * size : 3 * size, :], left) + fx_ref[size:, :].astype(F32)
    ).astype(BF)
    x_ref[2 * size :, :] = (dot(t_ref[:size, :], right) + fy_ref[:size, :].astype(F32)).astype(BF)
    kl_ref[...] = dot(t_ref[3 * size :, :], left) + fx_ref[:size, :].astype(F32)
    kr_ref[...] = dot(t_ref[3 * size :, :], right) + fy_ref[size:, :].astype(F32)


def second_kernel(
    t_ref, q1_ref, q2_ref, key_ref, value_ref, ex_ref, ey_ref, lx_ref, ly_ref, e_ref, o_ref,
    x_ref, y_ref, kl_ref, kr_ref,
):
    size = t_ref.shape[0] // 4

    def term(place, query_ref, other_ref, extra, early_ref, late_ref, half):
        block = t_ref[place * size : (place + 1) * size, :]
        here = slice(half * size, (half + 1) * size)
        early, late = early_ref[here, :].astype(F32), late_ref[here, :].astype(F32)
        return jnp.concatenate(
            [
                dot(block, query_ref[...]) + early[:, :PAIR],
                dot(block, other_ref[...]) + late,
                extra + early[:, PAIR:],
            ],
            axis=1,
        )

    y_ref[...] = term(2, q1_ref, key_ref, e_ref[0], ex_ref, lx_ref, 1).astype(BF)
    x_ref[...] = term(0, q2_ref, value_ref, o_ref[0], ey_ref, ly_ref, 0).astype(BF)
    kl_ref[...] = term(3, q1_ref, key_ref, e_ref[1], ex_ref, lx_ref, 0)
    kr_ref[...] = term(3, q2_ref, value_ref, o_ref[1], ey_ref, ly_ref, 1)


def gate(value, *others):
    return lax.optimization_barrier((value,) + others)[0]


def pick_groups(array, axis, unit, core):
    size = array.shape[axis]
    picked = [
        jnp.where(
            core == 0,
            lax.slice_in_dim(array, at, at + unit, axis=axis),
            lax.slice_in_dim(array, at + unit, at + 2 * unit, axis=axis),
        )
        for at in range(0, size, 2 * unit)
    ]
    return jnp.concatenate(picked, axis=axis)


def spread_groups(array, axis, unit, core):
    groups = jnp.split(array, array.shape[axis] // unit, axis=axis)
    parts = []
    for group in groups:
        empty = jnp.zeros_like(group)
        parts += [jnp.where(core == 0, group, empty), jnp.where(core == 0, empty, group)]
    return jnp.concatenate(parts, axis=axis)


def in_order(core, own, other, axis):
    first = jnp.where(core == 0, own, other)
    second = jnp.where(core == 0, other, own)
    return jnp.concatenate([first, second], axis=axis)


def xor_blocks(blocks, index):
    odd = (index & 1) == 1
    high = (index & 2) == 2
    near = [jnp.where(odd, blocks[k ^ 1], blocks[k]) for k in range(4)]
    return [jnp.where(high, near[k ^ 2], near[k]) for k in range(4)]


ORDER = (1, 3, 2, 0)
CHUNKS = ((0, 3), (1, 2))


def square(value, step):
    return lax.ppermute(value, "fsdp", [(i, i ^ step) for i in range(4)])


def chips(value, step, n_vox):
    return lax.ppermute(value, "vox", [(i, i ^ (2 * step)) for i in range(n_vox)])


def on_device(
    tokens, gain, w_qkv, w_out, logit_scale, key_blocks, slot_count, valid_voxels, cotangent
):
    own_tokens = tokens[0]
    own_cotangent = cotangent[0]
    own_rows, model_width = own_tokens.shape
    rows = 2 * own_rows
    own_blocks = key_blocks.shape[1]
    blocks = 2 * own_blocks
    slot_total = key_blocks.shape[2]
    reach = own_blocks // 2
    margin = reach * BLK
    n_vox = lax.axis_size("vox")
    n_fsdp = lax.axis_size("fsdp")
    n_chip = n_vox // 2
    place = lax.axis_index("vox")
    scene = lax.axis_index("fsdp")
    core = place % 2
    chip = place // 2
    fast = n_vox == 8 and n_fsdp == 4
    unit = 128 if fast else 64
    swap = [(i, i ^ 1) for i in range(n_vox)]
    even, low = chip % 2 == 0, chip < 2
    even_flag, core_flag, scene_flag = [
        jnp.reshape(x, (1,)).astype(jnp.int32) for x in (even, core, scene)
    ]
    near_chips = [(i, i ^ 2) for i in range(n_vox)]
    far_chips = []
    for i in range(n_vox):
        to = i // 2 + (1 if i // 2 % 2 else -1)
        far_chips.append((i, 2 * to + i % 2 if 0 <= to < n_chip else i))
    part_width = model_width // 2

    def columns_of(array, pairs):
        return jnp.concatenate(
            [
                array[:, base + p * PAIR : base + (p + 1) * PAIR]
                for base in range(0, array.shape[1], part_width)
                for p in pairs
            ],
            axis=1,
        )

    if fast:
        top, low_half = pick_weights(w_qkv, w_out, core_flag)
        far_top, near_low = square(top, 2), square(low_half, 1)
        near_top, far_low = square(top, 1), square(low_half, 2)
        diag_top, diag_low = square(far_top, 1), square(near_low, 2)
        near, diag = (near_top, near_low), (diag_top, diag_low)
        far, shard = (far_top, far_low), (top, low_half)
        wide = 3 * part_width // 2
        weights_0, weights_1 = [
            jnp.concatenate(
                [block[:, at : at + wide] for both in (near, diag, far, shard) for block in both],
                axis=0,
            )
            for at in (0, wide)
        ]
        wide = 2 * wide
        out_blocks = [
            jnp.concatenate([block[0][:, wide:], block[1][:, wide:]], axis=1)
            for block in (shard, near, far, diag)
        ]
        out_half = jnp.concatenate(xor_blocks(out_blocks, scene), axis=0)
    else:
        core_qkv = pick_groups(w_qkv, 1, unit, core)
        core_out = pick_groups(w_out, 0, unit, core)
        weights_0, weights_1 = [
            lax.all_gather(columns_of(core_qkv, pairs), "fsdp", axis=0, tiled=True)
            for pairs in CHUNKS
        ]
        out_half = lax.all_gather(core_out, "fsdp", axis=0, tiled=True)

    other_tokens = lax.ppermute(own_tokens, "vox", swap)
    other_cotangent = lax.ppermute(own_cotangent, "vox", swap)
    lists = jnp.concatenate([key_blocks[0], slot_count[0][:, None]], axis=1)
    all_lists = in_order(
        core, lists, lax.ppermute(lists.astype(F32), "vox", swap).astype(jnp.int32), 0
    )
    chip_tokens = in_order(core, own_tokens, other_tokens, 0)
    chip_cotangent = in_order(core, own_cotangent, other_cotangent, 0)

    first_block = chip * blocks
    pool_blocks = blocks + 2 * reach
    window_id = (
        all_lists[:, :slot_total] - first_block + reach
        - 2 * (jnp.arange(blocks, dtype=jnp.int32) // 2)[:, None]
    )
    used = jnp.arange(slot_total, dtype=jnp.int32)[None, :] < all_lists[:, slot_total:]
    hits = jnp.logical_and(
        window_id[:, :, None] == jnp.arange(WINDOW, dtype=jnp.int32), used[:, :, None]
    )
    mult = jnp.sum(hits.astype(jnp.int32), axis=1)
    scene_total = valid_voxels.shape[1]
    pool_ids = first_block - reach + jnp.arange(pool_blocks, dtype=jnp.int32)
    valid = jnp.take(valid_voxels[0], jnp.clip(pool_ids, 0, scene_total - 1))
    group_heads = unit // HD
    scales = pick_groups(logit_scale, 0, group_heads, core)

    wide = chip_tokens.astype(F32)
    inverse = lax.rsqrt(jnp.mean(wide * wide, axis=1, keepdims=True) + EPS)
    normed = (wide * inverse * gain).astype(BF)
    if fast:
        turned = xor_blocks(jnp.split(normed, 4, axis=1), scene)
        normed = jnp.concatenate([turned[k] for k in ORDER], axis=1)
        normed_t = small_kernel(turn_kernel, "turn", [], [normed], [(normed.shape[::-1], BF)])[0]

    def pairings(first, second):
        return lax.ppermute(first, "vox", near_chips), lax.ppermute(second, "vox", far_chips)

    def heads_of(packed, upstream, chunk, begin=0, count=2, carried=()):
        pairs = CHUNKS[chunk]
        used = pairs[begin : begin + count]
        chunk_scales = jnp.concatenate([scales[2 * p : 2 * p + 2] for p in used])
        return attention(
            packed, *halos, upstream, mult, valid, chunk_scales, even_flag, pairs, begin, count,
            4 * chunk, carried,
        )

    def with_rims(grad, first, second):
        first, second = first.astype(F32), second.astype(F32)
        return jnp.concatenate(
            [
                grad[:margin] + jnp.where(even, second, first),
                grad[margin : rows - margin],
                grad[rows - margin :] + jnp.where(even, first, second),
            ],
            axis=0,
        ).astype(BF)

    def key_value_grads(keys, values, rims):
        return [with_rims(g, rims[0][i], rims[1][i]) for i, g in enumerate((keys, values))]

    def out_rows(pairs):
        return jnp.concatenate([out_half[p * PAIR : (p + 1) * PAIR] for p in pairs], axis=0)

    def groups_of(left, right, chunk):
        half = 3 * PAIR
        groups = [left[:, k * PAIR : (k + 1) * PAIR] for k in range(3)]
        groups += [right[:, k * PAIR : (k + 1) * PAIR] for k in range(3)]
        sets = ((0, 3, 4), (1, 2, 5)) if chunk == 0 else ((0, 3, 2), (1, 4, 5))
        evens = jnp.concatenate([groups[k] for k in sets[0]] + [left[:, half:]], axis=1)
        odds = jnp.concatenate([groups[k] for k in sets[1]] + [right[:, half:]], axis=1)
        return jnp.where(even, evens, odds), jnp.where(even, odds, evens).astype(BF)

    def halves_of(kept):
        left, right = kept[:, : 2 * PAIR], kept[:, PAIR : 3 * PAIR]
        if kept.shape[1] > 3 * PAIR:
            more = kept[:, 3 * PAIR :]
            cut = more.shape[0] // 2
            left = jnp.concatenate([left, more[:cut]], axis=0)
            right = jnp.concatenate([right, more[cut:]], axis=0)
        return jnp.where(low, left, right), jnp.where(low, right, left).astype(BF)

    packed_0, packed_1 = [dot(normed, weight).astype(BF) for weight in (weights_0, weights_1)]
    query_width = part_width // 2
    top, bottom = [
        jnp.concatenate([packed[at, query_width:] for packed in (packed_0, packed_1)], axis=1)
        for at in (slice(0, margin), slice(rows - margin, rows))
    ]
    halos = pairings(jnp.where(even, bottom, top), jnp.where(even, top, bottom))
    upstream = dot(chip_cotangent, out_half, ((1,), (1,))).astype(BF)
    first = heads_of(packed_0, upstream, 0)
    rims_0 = pairings(first[4], first[5])
    third = heads_of(packed_1, gate(upstream, first[4], first[5]), 1, 0, 1)
    rims_0 = [gate(rim, third[6]) for rim in rims_0]
    half = 3 * query_width // 2
    if fast:
        left_0, right_0, to_x, to_y = small_kernel(
            rim_kernel, "rims_first", [even_flag],
            [normed_t, *rims_0, first[1], first[2], first[3]],
            [((rows, half), BF)] * 2 + [((model_width // 2, half), BF)] * 2,
        )
        from_x0, from_y0 = square(to_x, 1), square(to_y, 2)
        fourth_in = gate(upstream, to_x, to_y)
    else:
        key_0, value_0 = key_value_grads(first[2], first[3], rims_0)
        grad_0 = jnp.concatenate([first[1], key_0, value_0], axis=1)
        fourth_in = upstream
    fourth = heads_of(packed_1, fourth_in, 1, 1, 1, (third[0], third[4], third[5]))
    rims_1 = pairings(fourth[4], fourth[5])

    att_0 = gate(first[0], fourth[6])
    att_1 = fourth[0]
    if fast:
        quarter = model_width // 4
        to_x, to_y, left, right, evens, odds = small_kernel(
            leave_kernel, "leave_early", [scene_flag],
            [normed_t, first[7], third[7], fourth[7], chip_cotangent, third[1], fourth[1],
             left_0, right_0, from_x0, from_y0],
            [((3 * quarter, half), BF)] * 2
            + [((quarter, half), F32)] * 2
            + [((2, quarter, quarter), F32)] * 2,
            [pltpu.VMEM((4, PAIR, rows), BF)],
        )
        early_x, early_y = square(to_x, 1), square(to_y, 2)
        rims_1 = lax.optimization_barrier((*rims_1, to_x, to_y))[:2]

    if fast:
        key_1, value_1, to_x, to_y = small_kernel(
            rim_kernel, "rims_second", [even_flag],
            [normed_t, *rims_1, third[2], fourth[2], third[3], fourth[3]],
            [((rows, query_width), BF)] * 2 + [((model_width // 2, query_width), BF)] * 2,
        )
        late_x, late_y = square(to_x, 1), square(to_y, 2)
        early_x, early_y, att_0, att_1 = lax.optimization_barrier(
            (early_x, early_y, att_0, att_1, to_x, to_y)
        )[:4]
        height = model_width // 4
        kept_0, sent = groups_of(
            left + early_y[2 * height :].astype(F32), right + early_x[2 * height :].astype(F32), 0
        )
        got_0 = chips(sent, 1, n_vox)
        to_x, to_y, left, right = small_kernel(
            second_kernel, "second_exchange", [],
            [normed_t, third[1], fourth[1], key_1, value_1, early_x, early_y, late_x, late_y, evens, odds],
            [((height, half + quarter), BF)] * 2 + [((height, half + quarter), F32)] * 2,
        )
        end_x, end_y = square(to_x, 1), square(to_y, 2)
        left_0, key_1, scale_first, got_0 = lax.optimization_barrier(
            (left_0, key_1, first[6], got_0, to_x, to_y)
        )[:4]
        grad_0 = jnp.concatenate([left_0, right_0], axis=1)
    else:
        key_1, value_1 = key_value_grads(
            *[jnp.concatenate([third[i], fourth[i]], axis=1) for i in (2, 3)], rims_1
        )
        scale_first = first[6]
    mixed_part = dot(att_0, out_rows(CHUNKS[0])) + dot(att_1, out_rows(CHUNKS[1]))
    grad_1 = jnp.concatenate([third[1], fourth[1], key_1, value_1], axis=1)

    ngrad_part = dot(grad_0, weights_0, ((1,), (1,))) + dot(grad_1, weights_1, ((1,), (1,)))
    mixed_mine = lax.dynamic_slice_in_dim(mixed_part, core * own_rows, own_rows, 0)
    mixed_theirs = lax.dynamic_slice_in_dim(mixed_part, (1 - core) * own_rows, own_rows, 0)
    mixed = (
        own_tokens.astype(F32) + (mixed_mine + lax.ppermute(mixed_theirs, "vox", swap))
    ).astype(BF)

    ngrad_mine = lax.dynamic_slice_in_dim(ngrad_part, core * own_rows, own_rows, 0)
    ngrad_theirs = lax.dynamic_slice_in_dim(ngrad_part, (1 - core) * own_rows, own_rows, 0)
    normed_grad = ngrad_mine + lax.ppermute(ngrad_theirs, "vox", swap)
    if fast:
        held = jnp.split(normed_grad, 4, axis=1)
        normed_grad = jnp.concatenate(
            xor_blocks([held[ORDER.index(k)] for k in range(4)], scene), axis=1
        )

    own_wide = own_tokens.astype(F32)
    own_inverse = lax.rsqrt(jnp.mean(own_wide * own_wide, axis=1, keepdims=True) + EPS)
    gain_grad = jnp.sum(normed_grad * own_wide * own_inverse, axis=0)
    scaled_grad = normed_grad * gain
    token_grad = (
        own_cotangent.astype(F32)
        + own_inverse
        * (
            scaled_grad
            - own_wide
            * own_inverse
            * own_inverse
            * jnp.mean(scaled_grad * own_wide, axis=1, keepdims=True)
        )
    ).astype(BF)

    scale_parts = {}
    for pairs, sums in zip(
        CHUNKS, (scale_first, jnp.concatenate([third[6], fourth[6]], axis=0))
    ):
        sums = jnp.sum(sums.reshape(2, 8, 2, PAIR), axis=(1, 3))
        for i, p in enumerate(pairs):
            scale_parts[p] = sums[i]
    scale_part = jnp.concatenate([scale_parts[p] for p in range(len(scale_parts))])
    scale_grad = spread_groups(scale_part, 0, group_heads, core)

    if fast:
        small = jnp.concatenate([gain_grad, scale_grad, jnp.zeros((112,), F32)]).reshape(9, 128)
        small = small + square(small, 1)
        small = small + square(small, 2)
        kept_0, sent = halves_of(kept_0 + got_0.astype(F32))
        got_0 = chips(sent, 2, n_vox)
        kept_1, sent = groups_of(left + end_y.astype(F32), right + end_x.astype(F32), 1)
        got_1 = chips(sent, 1, n_vox)
        small = small + lax.ppermute(small, "vox", swap)
        small = small + chips(small, 1, n_vox)
        kept_1, sent = halves_of(kept_1 + got_1.astype(F32))
        got_1 = chips(sent, 2, n_vox)
        small = small + chips(small, 2, n_vox)
        small = small.reshape(-1)
        summed_gain, summed_scale = small[:model_width], small[model_width : model_width + HEADS]
        kept_1 = kept_1 + got_1.astype(F32)
        qkv_sums = [kept_0 + got_0.astype(F32), kept_1[:height]]
        out_sum = kept_1[height:]
    else:
        out_sums = [dot(att, chip_cotangent, ((0,), (0,))) for att in (att_0, att_1)]
        qkv_sums = [dot(normed, grad, ((0,), (0,))) for grad in (grad_0, grad_1)]
        summed_gain, summed_scale = lax.psum((gain_grad, scale_grad), ("vox", "fsdp"))

    if fast:
        half = out_sum.shape[1] // 2
        first, second = out_sum[:, :half], out_sum[:, half:]
        out_other = lax.ppermute(jnp.where(core == 0, second, first), "vox", swap)
        summed_out = in_order(core, jnp.where(core == 0, first, second), out_other, 0)

        a0, a1 = qkv_sums[0][:, :PAIR], qkv_sums[0][:, PAIR:]
        b0, b1 = qkv_sums[1][:, :PAIR], qkv_sums[1][:, PAIR:]

        def by_chip(options):
            value = options[3]
            for k in range(3):
                value = jnp.where(chip == k, options[k], value)
            return value

        g0 = by_chip((a0, a0, b1, b0))
        g1 = by_chip((b0, a1, a0, b1))
        g2 = by_chip((b1, b0, a1, a1))
        got = lax.ppermute(jnp.where(core == 0, g2, g0), "vox", swap)
        summed_qkv = jnp.concatenate(
            [
                jnp.where(core == 0, g0, g1),
                got,
                jnp.where(core == 0, g1, g2),
            ],
            axis=1,
        )
    else:
        by_pair = {}
        cols = {}
        for pairs, out_total, qkv_total in zip(CHUNKS, out_sums, qkv_sums):
            for i, p in enumerate(pairs):
                by_pair[p] = out_total[i * PAIR : (i + 1) * PAIR]
                for j in range(3):
                    at = (2 * j + i) * PAIR
                    cols[4 * j + p] = qkv_total[:, at : at + PAIR]
        out_total = jnp.concatenate([by_pair[p] for p in range(4)], axis=0)
        qkv_total = jnp.concatenate([cols[k] for k in range(12)], axis=1)
        out_total = spread_groups(out_total, 0, unit, core)
        qkv_total = lax.psum_scatter(qkv_total, "fsdp", scatter_dimension=0, tiled=True)
        qkv_total = spread_groups(qkv_total, 1, unit, core)
        summed_qkv = lax.psum_scatter(qkv_total, "vox", scatter_dimension=1, tiled=True)
        out_total = lax.psum_scatter(out_total, "fsdp", scatter_dimension=0, tiled=True)
        summed_out = lax.psum_scatter(out_total, "vox", scatter_dimension=1, tiled=True)

    return (
        mixed[None],
        token_grad[None],
        summed_qkv,
        summed_out,
        summed_gain,
        summed_scale,
    )


def solution(mesh):
    return jax.shard_map(
        on_device,
        mesh=mesh,
        in_specs=(
            P("fsdp", "vox", None),
            P(),
            P("fsdp", None),
            P("fsdp", None),
            P(),
            P("fsdp", "vox", None),
            P("fsdp", "vox"),
            P("fsdp", None),
            P("fsdp", "vox", None),
        ),
        out_specs=(
            P("fsdp", "vox", None),
            P("fsdp", "vox", None),
            P("fsdp", "vox"),
            P("fsdp", "vox"),
            P(),
            P(),
        ),
        check_vma=False,
    )
```

profile of v0, /device:TPU:0, one launch (start us, length us, event | category | flops | bytes accessed | tf_op | source)
XLA Modules:
  0.0 194.5 jit_solution(15580786271098734448)
XLA Ops:
  3.4 3.0 %collective-permute-start.2 = (bf16[128,2048]{1,0:T(8,128)(2,1)S(1)}, bf16[128,2048]{1,0:T(8,128)(2,1)S(1)}, u32[]{:S(2)}, u32[]{:S(2)}) collective-permute-start(bf16[128,2048]{1,0:T(8,128)(2,1)S(1)} %get-tuple-element.65), channel_id=1, source_target_pairs={{0,1},{1,0},{2,3},{3,2},{4,5},{5,4},{6,7},{7,6},{8,9},{9,8},{10,11... | collective-permute-start | bytes 1572872 | tf_op jit(solution)/shard_map/ppermute | solution.py:472
  6.4 1.5 collective-permute-start.4
  11.0 10.3 %collective-permute-done.4 = bf16[128,2048]{1,0:T(8,128)(2,1)} collective-permute-done((bf16[128,2048]{1,0:T(8,128)(2,1)S(1)}, bf16[128,2048]{1,0:T(8,128)(2,1)}, u32[]{:S(2)}, u32[]{:S(2)}) %collective-permute-start.4) | collective-permute-done | bytes 524320 | tf_op jit(solution)/shard_map/ppermute | solution.py:472
  22.3 7.4 %collective-permute-done.3 = bf16[128,2048]{1,0:T(8,128)(2,1)} collective-permute-done((bf16[128,2048]{1,0:T(8,128)(2,1)S(1)}, bf16[128,2048]{1,0:T(8,128)(2,1)}, u32[]{:S(2)}, u32[]{:S(2)}) %collective-permute-start.3) | collective-permute-done | bytes 524320 | tf_op jit(solution)/shard_map/ppermute | solution.py:472
  29.6 1.7 collective-permute-start.5
  32.3 1.6 collective-permute-start.6
  39.2 3.7 %collective-permute-done.5 = bf16[128,2048]{1,0:T(8,128)(2,1)S(1)} collective-permute-done((bf16[128,2048]{1,0:T(8,128)(2,1)}, bf16[128,2048]{1,0:T(8,128)(2,1)S(1)}, u32[]{:S(2)}, u32[]{:S(2)}) %collective-permute-start.5) | collective-permute-done | bytes 524320 | tf_op jit(solution)/shard_map/ppermute | solution.py:472
  43.0 2.1 %collective-permute-done.6 = bf16[128,2048]{1,0:T(8,128)(2,1)S(1)} collective-permute-done((bf16[128,2048]{1,0:T(8,128)(2,1)}, bf16[128,2048]{1,0:T(8,128)(2,1)S(1)}, u32[]{:S(2)}, u32[]{:S(2)}) %collective-permute-start.6) | collective-permute-done | bytes 524320 | tf_op jit(solution)/shard_map/ppermute | solution.py:472
  49.6 1.6 collective-permute-start.8
  53.6 4.8 %collective-permute-done.8.k1_ref.v1_ref = bf16[192,1024]{1,0:T(8,128)(2,1)S(1)} collective-permute-done((bf16[192,1024]{1,0:T(8,128)(2,1)S(1)}, bf16[192,1024]{1,0:T(8,128)(2,1)S(1)}, u32[]{:S(2)}, u32[]{:S(2)}) %collective-permute-start.8) | collective-permute-done | bytes 393248 | tf_op jit(solution)/shard_map/ppermute | solution.py:587
  58.5 11.8 %block_attention.3 = (bf16[768,256]{1,0:T(8,128)(2,1)S(1)}, bf16[768,256]{1,0:T(8,128)(2,1)S(1)}, f32[768,256]{1,0:T(8,128)S(1)}, f32[768,256]{1,0:T(8,128)S(1)}...) custom-call(s32[12,8]{1,0:T(8,128)S(1)} %copy.23.mult_ref, ...), custom_call_target="tpu_custom_call" | custom-call | flops 19327352832 | bytes 3932160 | tf_op jit(solution)/shard_map/block_attention/pallas_call | solution.py:216
  71.0 4.6 %collective-permute-start.11 = (bf16[2,192,256]{2,1,0:T(8,128)(2,1)S(1)}, bf16[2,192,256]{2,1,0:T(8,128)(2,1)S(1)}, u32[]{:S(2)}, u32[]{:S(2)}) collective-permute-start(bf16[2,192,256]{2,1,0:T(8,128)(2,1)S(1)} %get-tuple-element.68), channel_id=1, source_target_pairs={{0,8},{4,12},{8,0},{12,4},{16,24},{20,28},{24,16},{28,20},{1,9},{5... | collective-permute-start | bytes 589832 | tf_op jit(solution)/shard_map/ppermute | solution.py:587
  77.8 5.7 %block_attention.4 = (bf16[768,128]{1,0:T(8,128)(2,1)S(1)}, bf16[768,128]{1,0:T(8,128)(2,1)S(1)}, f32[768,128]{1,0:T(8,128)S(1)}, f32[768,128]{1,0:T(8,128)S(1)}...) custom-call(s32[12,8]{1,0:T(8,128)S(1)} %copy-done.27, ...), custom_call_target="tpu_custom_call" | custom-call | flops 9663676416 | bytes 1966080 | tf_op jit(solution)/shard_map/block_attention/pallas_call | solution.py:216
  86.0 1.5 collective-permute-start.14
  87.5 6.6 %block_attention.5 = (bf16[768,256]{1,0:T(8,128)(2,1)S(1)}, bf16[768,128]{1,0:T(8,128)(2,1)S(1)}, f32[768,128]{1,0:T(8,128)S(1)}, f32[768,128]{1,0:T(8,128)S(1)}...) custom-call(s32[12,8]{1,0:T(8,128)S(1)} %copy-done.27, ...), custom_call_target="tpu_custom_call" | custom-call | flops 9663676416 | bytes 1966080 | tf_op jit(solution)/shard_map/block_attention/pallas_call | solution.py:216
  94.9 3.2 %leave_early.1 = (bf16[768,384]{1,0:T(8,128)(2,1)}, bf16[768,384]{1,0:T(8,128)(2,1)}, f32[256,384]{1,0:T(8,128)S(1)}, f32[256,384]{1,0:T(8,128)S(1)}, f32[2,256,...) custom-call(s32[1]{0:T(128)} %bitcast.1.scene_ref, bf16[1024,768]{1,0:T(8,128)(2,1)S(1)} %turn.1.refs_0_.t_ref, ...), custom_call_target="tpu_custom_call" | custom-call | tf_op jit(solution)/shard_map/leave_early/pallas_call | solution.py:303
  104.1 3.0 %collective-permute-start.17 = (bf16[2,192,256]{2,1,0:T(8,128)(2,1)}, bf16[2,192,256]{2,1,0:T(8,128)(2,1)}, u32[]{:S(2)}, u32[]{:S(2)}) collective-permute-start(bf16[2,192,256]{2,1,0:T(8,128)(2,1)} %get-tuple-element.95), channel_id=1, source_target_pairs={{0,8},{4,12},{8,0},{12,4},{16,24},{20,28},{24,16},{28,20},{1,9},{5... | collective-permute-start | bytes 589832 | tf_op jit(solution)/shard_map/ppermute | solution.py:587
  107.1 3.0 %collective-permute-start.18 = (bf16[2,192,256]{2,1,0:T(8,128)(2,1)}, bf16[2,192,256]{2,1,0:T(8,128)(2,1)}, u32[]{:S(2)}, u32[]{:S(2)}) collective-permute-start(bf16[2,192,256]{2,1,0:T(8,128)(2,1)} %get-tuple-element.96), channel_id=1, source_target_pairs={{0,0},{4,4},{8,16},{12,20},{16,8},{20,12},{24,24},{28,28},{1,1},{5... | collective-permute-start | bytes 589832 | tf_op jit(solution)/shard_map/ppermute | solution.py:587
  118.6 1.7 rims_second.1
  127.8 2.2 %second_exchange.1 = (bf16[256,640]{1,0:T(8,128)(2,1)S(1)}, bf16[256,640]{1,0:T(8,128)(2,1)S(1)}, f32[256,640]{1,0:T(8,128)S(1)}, f32[256,640]{1,0:T(8,128)S(1)}) custom-call(bf16[1024,768]{1,0:T(8,128)(2,1)S(1)} %turn.1.refs_0_.t_ref, bf16[768,128]{1,0:T(8,128)(2,1)S(1)} %get-tuple-element.85.q1_ref, bf16[768,128]{1,0:T(8,128)(2,1)S(1)} %copy-done.4, ...), custom_call_target="tpu_custom_call" | custom-call | tf_op jit(solution)/shard_map/second_exchange/pallas_call | solution.py:303
  130.0 1.6 collective-permute-start.25
  137.7 3.6 %collective-permute-done.24 = bf16[256,640]{1,0:T(8,128)(2,1)S(1)} collective-permute-done((bf16[256,640]{1,0:T(8,128)(2,1)S(1)}, bf16[256,640]{1,0:T(8,128)(2,1)S(1)}, u32[]{:S(2)}, u32[]{:S(2)}) %collective-permute-start.24) | collective-permute-done | bytes 327712 | tf_op jit(solution)/shard_map/ppermute | solution.py:472
  143.2 1.7 collective-permute-start.26
  148.1 6.9 %collective-permute-done.26 = bf16[256,640]{1,0:T(8,128)(2,1)S(1)} collective-permute-done((bf16[256,640]{1,0:T(8,128)(2,1)S(1)}, bf16[256,640]{1,0:T(8,128)(2,1)S(1)}, u32[]{:S(2)}, u32[]{:S(2)}) %collective-permute-start.26) | collective-permute-done | bytes 327712 | tf_op jit(solution)/shard_map/ppermute | solution.py:476
  157.3 8.3 %collective-permute-done.27 = bf16[384,256]{1,0:T(8,128)(2,1)S(1)} collective-permute-done((bf16[384,256]{1,0:T(8,128)(2,1)S(1)}, bf16[384,256]{1,0:T(8,128)(2,1)S(1)}, u32[]{:S(2)}, u32[]{:S(2)}) %collective-permute-start.27) | collective-permute-done | bytes 196640 | tf_op jit(solution)/shard_map/ppermute | solution.py:476
  171.2 3.5 %fusion.7 = (f32[1024]{0:T(1024)S(1)}, f32[384]{0:T(512)}, bf16[1,384,1024]{2,1,0:T(8,128)(2,1)}) fusion(f32[384,256]{1,0:T(8,128)S(1)} %get-tuple-element.134, f32[384,256]{1,0:T(8,128)S(1)} %get-tuple-element.133, f32[384,256]{1,0:T(8,128)S(1)} %get-tuple-element.132, f32[384,256]{1,0:T(8,128)S(1)} %get-tuple-element.131, f32[384]{0:T(512)S(1)} %copy-done.61, ...), kind=kLoop, calls=%fused_computation.16 | loop fusion | flops 5110400 | bytes 6302724 | tf_op jit(solution)/shard_map/reduce_sum | solution.py:728
  177.4 2.3 %collective-permute-done.31 = f32[9,128]{1,0:T(8,128)S(1)} collective-permute-done((f32[9,128]{1,0:T(8,128)S(1)}, f32[9,128]{1,0:T(8,128)S(1)}, u32[]{:S(2)}, u32[]{:S(2)}) %collective-permute-start.31) | collective-permute-done | bytes 4640 | tf_op jit(solution)/shard_map/ppermute | solution.py:472
  180.6 2.8 %collective-permute-done.32 = f32[9,128]{1,0:T(8,128)S(1)} collective-permute-done((f32[9,128]{1,0:T(8,128)S(1)}, f32[9,128]{1,0:T(8,128)S(1)}, u32[]{:S(2)}, u32[]{:S(2)}) %collective-permute-start.32) | collective-permute-done | bytes 4640 | tf_op jit(solution)/shard_map/ppermute | solution.py:472
  183.3 1.8 pad_maximum_fusion.12
  185.8 3.0 %collective-permute-done.34 = f32[9,128]{1,0:T(8,128)S(1)} collective-permute-done((f32[9,128]{1,0:T(8,128)S(1)}, f32[9,128]{1,0:T(8,128)S(1)}, u32[]{:S(2)}, u32[]{:S(2)}) %collective-permute-start.34) | collective-permute-done | bytes 4640 | tf_op jit(solution)/shard_map/ppermute | solution.py:476
  189.6 2.1 %fusion.11 = bf16[1,384,1024]{2,1,0:T(8,128)(2,1)} fusion(f32[1,384,256]{2,1,0:T(8,128)S(1)} %bitcast.60, f32[1,384,256]{2,1,0:T(8,128)S(1)} %bitcast.59, f32[1,384,256]{2,1,0:T(8,128)S(1)} %bitcast.58, f32[1,384,256]{2,1,0:T(8,128)S(1)} %bitcast.57, bf16[1,384,1024]{2,1,0:T(8,128)(2,1)S(1)} %copy-done.39, bf16[1,384,1024]{2,1,0:T(8,128)(2,1)S(1)} %copy-done.41, ...), kind=kLoop, calls=%fused_computation.24 | loop fusion | flops 5111808 | bytes 3939328 | tf_op jit(solution)/shard_map/convert_element_type | solution.py:740
  191.7 1.7 collective-permute-done.35
  (282 shorter events, 72.3 us)
Async XLA Ops:
  3.4 30.6 %collective-permute-start.2 = (bf16[128,2048]{1,0:T(8,128)(2,1)S(1)}, bf16[128,2048]{1,0:T(8,128)(2,1)S(1)}, u32[]{:S(2)}, u32[]{:S(2)}) collective-permute-start(bf16[128,2048]{1,0:T(8,128)(2,1)S(1)} %get-tuple-element.65), channel_id=1, source_target_pairs={{0,1},{1,0},{2,3},{3,2},{4,5},{5,4},{6,7},{7,6},{8,9},{9,8},{10,11... | collective-permute-start | bytes 1572872 | tf_op jit(solution)/shard_map/ppermute | solution.py:472
  6.4 15.0 %collective-permute-start.4 = (bf16[128,2048]{1,0:T(8,128)(2,1)S(1)}, bf16[128,2048]{1,0:T(8,128)(2,1)}, u32[]{:S(2)}, u32[]{:S(2)}) collective-permute-start(bf16[128,2048]{1,0:T(8,128)(2,1)S(1)} %get-tuple-element.65), channel_id=1, source_target_pairs={{0,2},{1,3},{2,0},{3,1},{4,6},{5,7},{6,4},{7,5},{8,10},{9,11},{10,... | collective-permute-start | bytes 1572872 | tf_op jit(solution)/shard_map/ppermute | solution.py:472
  7.9 21.7 %collective-permute-start.3 = (bf16[128,2048]{1,0:T(8,128)(2,1)S(1)}, bf16[128,2048]{1,0:T(8,128)(2,1)}, u32[]{:S(2)}, u32[]{:S(2)}) collective-permute-start(bf16[128,2048]{1,0:T(8,128)(2,1)S(1)} %get-tuple-element.66), channel_id=1, source_target_pairs={{0,1},{1,0},{2,3},{3,2},{4,5},{5,4},{6,7},{7,6},{8,9},{9,8},{10,11... | collective-permute-start | bytes 1572872 | tf_op jit(solution)/shard_map/ppermute | solution.py:472
  8.4 23.9 %collective-permute-start.7 = (bf16[128,2048]{1,0:T(8,128)(2,1)S(1)}, bf16[128,2048]{1,0:T(8,128)(2,1)S(1)}, u32[]{:S(2)}, u32[]{:S(2)}) collective-permute-start(bf16[128,2048]{1,0:T(8,128)(2,1)S(1)} %get-tuple-element.66), channel_id=1, source_target_pairs={{0,2},{1,3},{2,0},{3,1},{4,6},{5,7},{6,4},{7,5},{8,10},{9,11},{10,... | collective-permute-start | bytes 1572872 | tf_op jit(solution)/shard_map/ppermute | solution.py:472
  10.2 24.8 %collective-permute-start = (bf16[384,1024]{1,0:T(8,128)(2,1)S(1)}, bf16[384,1024]{1,0:T(8,128)(2,1)}, u32[]{:S(2)}, u32[]{:S(2)}) collective-permute-start(bf16[384,1024]{1,0:T(8,128)(2,1)S(1)} %bitcast.56), channel_id=1, source_target_pairs={{0,4},{4,0},{8,12},{12,8},{16,20},{20,16},{24,28},{28,24},{1,5},{5... | collective-permute-start | bytes 2359304 | tf_op jit(solution)/shard_map/ppermute | solution.py:552
  21.3 16.1 %collective-permute-start.10 = (bf16[384,1024]{1,0:T(8,128)(2,1)}, bf16[384,1024]{1,0:T(8,128)(2,1)S(1)}, u32[]{:S(2)}, u32[]{:S(2)}) collective-permute-start(bf16[384,1024]{1,0:T(8,128)(2,1)} %bitcast.61), channel_id=1, source_target_pairs={{0,4},{4,0},{8,12},{12,8},{16,20},{20,16},{24,28},{28,24},{1,5},{5... | collective-permute-start | bytes 2359304 | tf_op jit(solution)/shard_map/ppermute | solution.py:553
  29.6 13.3 %collective-permute-start.5 = (bf16[128,2048]{1,0:T(8,128)(2,1)}, bf16[128,2048]{1,0:T(8,128)(2,1)S(1)}, u32[]{:S(2)}, u32[]{:S(2)}) collective-permute-start(bf16[128,2048]{1,0:T(8,128)(2,1)} %collective-permute-done.4), channel_id=1, source_target_pairs={{0,1},{1,0},{2,3},{3,2},{4,5},{5,4},{6,7},{7,6},{8,9},{9,8},{10,11... | collective-permute-start | bytes 1572872 | tf_op jit(solution)/shard_map/ppermute | solution.py:472
  32.3 12.8 %collective-permute-start.6 = (bf16[128,2048]{1,0:T(8,128)(2,1)}, bf16[128,2048]{1,0:T(8,128)(2,1)S(1)}, u32[]{:S(2)}, u32[]{:S(2)}) collective-permute-start(bf16[128,2048]{1,0:T(8,128)(2,1)} %collective-permute-done.3), channel_id=1, source_target_pairs={{0,2},{1,3},{2,0},{3,1},{4,6},{5,7},{6,4},{7,5},{8,10},{9,11},{10,... | collective-permute-start | bytes 1572872 | tf_op jit(solution)/shard_map/ppermute | solution.py:472
  49.6 8.8 %collective-permute-start.8 = (bf16[192,1024]{1,0:T(8,128)(2,1)S(1)}, bf16[192,1024]{1,0:T(8,128)(2,1)S(1)}, u32[]{:S(2)}, u32[]{:S(2)}) collective-permute-start(bf16[192,1024]{1,0:T(8,128)(2,1)S(1)} %get-tuple-element.153), channel_id=1, source_target_pairs={{0,8},{4,12},{8,0},{12,4},{16,24},{20,28},{24,16},{28,20},{1,9},{5... | collective-permute-start | bytes 1179656 | tf_op jit(solution)/shard_map/ppermute | solution.py:587
  51.2 7.2 %collective-permute-start.9 = (bf16[192,1024]{1,0:T(8,128)(2,1)S(1)}, bf16[192,1024]{1,0:T(8,128)(2,1)S(1)}, u32[]{:S(2)}, u32[]{:S(2)}) collective-permute-start(bf16[192,1024]{1,0:T(8,128)(2,1)S(1)} %get-tuple-element.152), channel_id=1, source_target_pairs={{0,0},{4,4},{8,16},{12,20},{16,8},{20,12},{24,24},{28,28},{1,1},{5... | collective-permute-start | bytes 1179656 | tf_op jit(solution)/shard_map/ppermute | solution.py:587
  71.0 13.3 %collective-permute-start.11 = (bf16[2,192,256]{2,1,0:T(8,128)(2,1)S(1)}, bf16[2,192,256]{2,1,0:T(8,128)(2,1)S(1)}, u32[]{:S(2)}, u32[]{:S(2)}) collective-permute-start(bf16[2,192,256]{2,1,0:T(8,128)(2,1)S(1)} %get-tuple-element.68), channel_id=1, source_target_pairs={{0,8},{4,12},{8,0},{12,4},{16,24},{20,28},{24,16},{28,20},{1,9},{5... | collective-permute-start | bytes 589832 | tf_op jit(solution)/shard_map/ppermute | solution.py:587
  75.6 8.7 %collective-permute-start.12 = (bf16[2,192,256]{2,1,0:T(8,128)(2,1)S(1)}, bf16[2,192,256]{2,1,0:T(8,128)(2,1)S(1)}, u32[]{:S(2)}, u32[]{:S(2)}) collective-permute-start(bf16[2,192,256]{2,1,0:T(8,128)(2,1)S(1)} %get-tuple-element.69), channel_id=1, source_target_pairs={{0,0},{4,4},{8,16},{12,20},{16,8},{20,12},{24,24},{28,28},{1,1},{5... | collective-permute-start | bytes 589832 | tf_op jit(solution)/shard_map/ppermute | solution.py:587
  85.4 9.5 %collective-permute-start.13 = (bf16[512,384]{1,0:T(8,128)(2,1)S(1)}, bf16[512,384]{1,0:T(8,128)(2,1)S(1)}, u32[]{:S(2)}, u32[]{:S(2)}) collective-permute-start(bf16[512,384]{1,0:T(8,128)(2,1)S(1)} %get-tuple-element.78), channel_id=1, source_target_pairs={{0,1},{1,0},{2,3},{3,2},{4,5},{5,4},{6,7},{7,6},{8,9},{9,8},{10,11... | collective-permute-start | bytes 1179656 | tf_op jit(solution)/shard_map/ppermute | solution.py:472
  86.0 8.9 %collective-permute-start.14 = (bf16[512,384]{1,0:T(8,128)(2,1)S(1)}, bf16[512,384]{1,0:T(8,128)(2,1)S(1)}, u32[]{:S(2)}, u32[]{:S(2)}) collective-permute-start(bf16[512,384]{1,0:T(8,128)(2,1)S(1)} %get-tuple-element.79), channel_id=1, source_target_pairs={{0,2},{1,3},{2,0},{3,1},{4,6},{5,7},{6,4},{7,5},{8,10},{9,11},{10,... | collective-permute-start | bytes 1179656 | tf_op jit(solution)/shard_map/ppermute | solution.py:472
  101.3 21.2 %collective-permute-start.15 = (bf16[768,384]{1,0:T(8,128)(2,1)}, bf16[768,384]{1,0:T(8,128)(2,1)S(1)}, u32[]{:S(2)}, u32[]{:S(2)}) collective-permute-start(bf16[768,384]{1,0:T(8,128)(2,1)} %get-tuple-element.89), channel_id=1, source_target_pairs={{0,1},{1,0},{2,3},{3,2},{4,5},{5,4},{6,7},{7,6},{8,9},{9,8},{10,11... | collective-permute-start | bytes 1769480 | tf_op jit(solution)/shard_map/ppermute | solution.py:472
  102.8 19.7 %collective-permute-start.16 = (bf16[768,384]{1,0:T(8,128)(2,1)}, bf16[768,384]{1,0:T(8,128)(2,1)}, u32[]{:S(2)}, u32[]{:S(2)}) collective-permute-start(bf16[768,384]{1,0:T(8,128)(2,1)} %get-tuple-element.90), channel_id=1, source_target_pairs={{0,2},{1,3},{2,0},{3,1},{4,6},{5,7},{6,4},{7,5},{8,10},{9,11},{10,... | collective-permute-start | bytes 1769480 | tf_op jit(solution)/shard_map/ppermute | solution.py:472
  104.1 10.5 %collective-permute-start.17 = (bf16[2,192,256]{2,1,0:T(8,128)(2,1)}, bf16[2,192,256]{2,1,0:T(8,128)(2,1)}, u32[]{:S(2)}, u32[]{:S(2)}) collective-permute-start(bf16[2,192,256]{2,1,0:T(8,128)(2,1)} %get-tuple-element.95), channel_id=1, source_target_pairs={{0,8},{4,12},{8,0},{12,4},{16,24},{20,28},{24,16},{28,20},{1,9},{5... | collective-permute-start | bytes 589832 | tf_op jit(solution)/shard_map/ppermute | solution.py:587
  107.1 7.5 %collective-permute-start.18 = (bf16[2,192,256]{2,1,0:T(8,128)(2,1)}, bf16[2,192,256]{2,1,0:T(8,128)(2,1)}, u32[]{:S(2)}, u32[]{:S(2)}) collective-permute-start(bf16[2,192,256]{2,1,0:T(8,128)(2,1)} %get-tuple-element.96), channel_id=1, source_target_pairs={{0,0},{4,4},{8,16},{12,20},{16,8},{20,12},{24,24},{28,28},{1,1},{5... | collective-permute-start | bytes 589832 | tf_op jit(solution)/shard_map/ppermute | solution.py:587
  120.3 7.3 %collective-permute-start.21 = (bf16[512,256]{1,0:T(8,128)(2,1)S(1)}, bf16[512,256]{1,0:T(8,128)(2,1)S(1)}, u32[]{:S(2)}, u32[]{:S(2)}) collective-permute-start(bf16[512,256]{1,0:T(8,128)(2,1)S(1)} %get-tuple-element.103), channel_id=1, source_target_pairs={{0,1},{1,0},{2,3},{3,2},{4,5},{5,4},{6,7},{7,6},{8,9},{9,8},{10,11... | collective-permute-start | bytes 786440 | tf_op jit(solution)/shard_map/ppermute | solution.py:472
  120.9 6.7 %collective-permute-start.22 = (bf16[512,256]{1,0:T(8,128)(2,1)S(1)}, bf16[512,256]{1,0:T(8,128)(2,1)S(1)}, u32[]{:S(2)}, u32[]{:S(2)}) collective-permute-start(bf16[512,256]{1,0:T(8,128)(2,1)S(1)} %get-tuple-element.104), channel_id=1, source_target_pairs={{0,2},{1,3},{2,0},{3,1},{4,6},{5,7},{6,4},{7,5},{8,10},{9,11},{10,... | collective-permute-start | bytes 786440 | tf_op jit(solution)/shard_map/ppermute | solution.py:472
  123.8 8.8 %collective-permute-start.20 = (bf16[256,384]{1,0:T(8,128)(2,1)S(1)}, bf16[256,384]{1,0:T(8,128)(2,1)S(1)}, u32[]{:S(2)}, u32[]{:S(2)}) collective-permute-start(bf16[256,384]{1,0:T(8,128)(2,1)S(1)} %select_convert_fusion.2), channel_id=1, source_target_pairs={{0,8},{4,12},{8,0},{12,4},{16,24},{20,28},{24,16},{28,20},{1,9},{5... | collective-permute-start | bytes 589832 | tf_op jit(solution)/shard_map/ppermute | solution.py:476
  127.6 41.8 %collective-permute-start.19 = (f32[384,1024]{1,0:T(8,128)}, f32[384,1024]{1,0:T(8,128)}, u32[]{:S(2)}, u32[]{:S(2)}) collective-permute-start(f32[384,1024]{1,0:T(8,128)} %constant_dynamic-slice_fusion.1), channel_id=1, source_target_pairs={{0,4},{4,0},{8,12},{12,8},{16,20},{20,16},{24,28},{28,24},{1,5},{5... | collective-permute-start | bytes 4718600 | tf_op jit(solution)/shard_map/ppermute | solution.py:714
  130.0 11.5 %collective-permute-start.25 = (bf16[256,640]{1,0:T(8,128)(2,1)S(1)}, bf16[256,640]{1,0:T(8,128)(2,1)S(1)}, u32[]{:S(2)}, u32[]{:S(2)}) collective-permute-start(bf16[256,640]{1,0:T(8,128)(2,1)S(1)} %get-tuple-element.116), channel_id=1, source_target_pairs={{0,1},{1,0},{2,3},{3,2},{4,5},{5,4},{6,7},{7,6},{8,9},{9,8},{10,11... | collective-permute-start | bytes 983048 | tf_op jit(solution)/shard_map/ppermute | solution.py:472
  131.5 9.8 %collective-permute-start.24 = (bf16[256,640]{1,0:T(8,128)(2,1)S(1)}, bf16[256,640]{1,0:T(8,128)(2,1)S(1)}, u32[]{:S(2)}, u32[]{:S(2)}) collective-permute-start(bf16[256,640]{1,0:T(8,128)(2,1)S(1)} %get-tuple-element.117), channel_id=1, source_target_pairs={{0,2},{1,3},{2,0},{3,1},{4,6},{5,7},{6,4},{7,5},{8,10},{9,11},{10,... | collective-permute-start | bytes 983048 | tf_op jit(solution)/shard_map/ppermute | solution.py:472
  137.6 31.3 %collective-permute-start.23 = (f32[384,1024]{1,0:T(8,128)}, f32[384,1024]{1,0:T(8,128)S(1)}, u32[]{:S(2)}, u32[]{:S(2)}) collective-permute-start(f32[384,1024]{1,0:T(8,128)} %constant_dynamic-slice_fusion), channel_id=1, source_target_pairs={{0,4},{4,0},{8,12},{12,8},{16,20},{20,16},{24,28},{28,24},{1,5},{5... | collective-permute-start | bytes 4718600 | tf_op jit(solution)/shard_map/ppermute | solution.py:719
  143.2 11.8 %collective-permute-start.26 = (bf16[256,640]{1,0:T(8,128)(2,1)S(1)}, bf16[256,640]{1,0:T(8,128)(2,1)S(1)}, u32[]{:S(2)}, u32[]{:S(2)}) collective-permute-start(bf16[256,640]{1,0:T(8,128)(2,1)S(1)} %select_convert_fusion), channel_id=1, source_target_pairs={{0,8},{4,12},{8,0},{12,4},{16,24},{20,28},{24,16},{28,20},{1,9},{5... | collective-permute-start | bytes 983048 | tf_op jit(solution)/shard_map/ppermute | solution.py:476
  145.6 10.8 %collective-permute-start.28 = (bf16[256,256]{1,0:T(8,128)(2,1)}, bf16[256,256]{1,0:T(8,128)(2,1)}, u32[]{:S(2)}, u32[]{:S(2)}) collective-permute-start(bf16[256,256]{1,0:T(8,128)(2,1)} %select_convert_fusion.3), channel_id=1, source_target_pairs={{0,16},{4,20},{8,24},{12,28},{16,0},{20,4},{24,8},{28,12},{1,17},{... | collective-permute-start | bytes 393224 | tf_op jit(solution)/shard_map/ppermute | solution.py:476
  156.3 9.4 %collective-permute-start.27 = (bf16[384,256]{1,0:T(8,128)(2,1)S(1)}, bf16[384,256]{1,0:T(8,128)(2,1)S(1)}, u32[]{:S(2)}, u32[]{:S(2)}) collective-permute-start(bf16[384,256]{1,0:T(8,128)(2,1)S(1)} %select_convert_fusion.1), channel_id=1, source_target_pairs={{0,16},{4,20},{8,24},{12,28},{16,0},{20,4},{24,8},{28,12},{1,17},{... | collective-permute-start | bytes 589832 | tf_op jit(solution)/shard_map/ppermute | solution.py:476
  167.1 16.2 %collective-permute-start.29 = (f32[256,128]{1,0:T(8,128)}, f32[256,128]{1,0:T(8,128)}, u32[]{:S(2)}, u32[]{:S(2)}) collective-permute-start(f32[256,128]{1,0:T(8,128)} %get-tuple-element.129), channel_id=1, source_target_pairs={{0,4},{4,0},{8,12},{12,8},{16,20},{20,16},{24,28},{28,24},{1,5},{5... | collective-permute-start | bytes 393224 | tf_op jit(solution)/shard_map/ppermute | solution.py:793
  167.8 8.8 %collective-permute-start.30 = (f32[128,128]{1,0:T(8,128)}, f32[128,128]{1,0:T(8,128)}, u32[]{:S(2)}, u32[]{:S(2)}) collective-permute-start(f32[128,128]{1,0:T(8,128)} %slice_select_fusion.4), channel_id=1, source_target_pairs={{0,4},{4,0},{8,12},{12,8},{16,20},{20,16},{24,28},{28,24},{1,5},{5... | collective-permute-start | bytes 196616 | tf_op jit(solution)/shard_map/ppermute | solution.py:778
  176.0 3.7 %collective-permute-start.31 = (f32[9,128]{1,0:T(8,128)S(1)}, f32[9,128]{1,0:T(8,128)S(1)}, u32[]{:S(2)}, u32[]{:S(2)}) collective-permute-start(f32[9,128]{1,0:T(8,128)S(1)} %bitcast.62), channel_id=1, source_target_pairs={{0,1},{1,0},{2,3},{3,2},{4,5},{5,4},{6,7},{7,6},{8,9},{9,8},{10,11... | collective-permute-start | bytes 13832 | tf_op jit(solution)/shard_map/ppermute | solution.py:472
  188.8 4.5 %collective-permute-start.35 = (f32[9,128]{1,0:T(8,128)S(1)}, f32[9,128]{1,0:T(8,128)S(1)}, u32[]{:S(2)}, u32[]{:S(2)}) collective-permute-start(f32[9,128]{1,0:T(8,128)S(1)} %add.175), channel_id=1, source_target_pairs={{0,16},{4,20},{8,24},{12,28},{16,0},{20,4},{24,8},{28,12},{1,17},{... | collective-permute-start | bytes 13832 | tf_op jit(solution)/shard_map/ppermute | solution.py:476
  (68 other events, 294.4 us)
where the time goes:
time: 196 us; the launch traced here: 194 us
  waiting for transfers between devices  57 us (29%)
  starting transfers between devices  36.5 us (19%)
  Pallas kernels  33 us (17%)
  local copies, waits for them, and re-layouts  31.1 us (16%)
  other arithmetic  27.3 us (14%)
  matrix products  7.77 us (4%)
    ppermute x16, waiting for transfers between devices, square(): return lax.ppermute(value, 'fsdp', [(i, i ^ step) for i in range(4)])  32.3 us
    pallas_call x3, Pallas kernels, attention(): pl.pallas_call(attention_kernel, grid_spec=pltpu.PrefetchScalarGridSpec(n...  24.1 us
    unnamed x135, local copies, waits for them, and re-layouts  20.2 us
    ppermute x6, waiting for transfers between devices, chips(): return lax.ppermute(value, 'vox', [(i, i ^ 2 * step) for i in range(n_vox)])  19.9 us
    ppermute x16, starting transfers between devices, square(): return lax.ppermute(value, 'fsdp', [(i, i ^ step) for i in range(4)])  18.1 us
    ppermute x3, starting transfers between devices, pairings(): lax.ppermute(first, 'vox', near_chips)  9.19 us
    pallas_call x6, Pallas kernels, small_kernel(): pl.pallas_call(kernel, grid_spec=pltpu.PrefetchScalarGridSpec(num_scalar_...  8.94 us
    dot_general x7, matrix products, dot(): return lax.dot_general(a, b, (dims, ((), ())), preferred_element_type=F32)  7.77 us
  transfers between devices with their start and end apart: 36, of which 12 were waited for; matrix products, arithmetic and copies ran while one was open for 22% of the time, Pallas kernels for 9%

commit v1 on v0

--- a/solution.py
+++ b/solution.py
@@ -522,8 +522,9 @@
     if fast:
         top, low_half = pick_weights(w_qkv, w_out, core_flag)
         far_top, near_low = square(top, 2), square(low_half, 1)
-        near_top, far_low = square(top, 1), square(low_half, 2)
         diag_top, diag_low = square(far_top, 1), square(near_low, 2)
+        later_top, later_low = lax.optimization_barrier((top, low_half, far_top, near_low))[:2]
+        near_top, far_low = square(later_top, 1), square(later_low, 2)
         near, diag = (near_top, near_low), (diag_top, diag_low)
         far, shard = (far_top, far_low), (top, low_half)
         wide = 3 * part_width // 2
@@ -662,9 +663,15 @@
     att_1 = fourth[0]
     if fast:
         quarter = model_width // 4
+        key_1, value_1, to_x, to_y = small_kernel(
+            rim_kernel, "rims_second", [even_flag],
+            [normed_t, *rims_1, third[2], fourth[2], third[3], fourth[3]],
+            [((rows, query_width), BF)] * 2 + [((model_width // 2, query_width), BF)] * 2,
+        )
+        late_x, late_y = square(to_x, 1), square(to_y, 2)
         to_x, to_y, left, right, evens, odds = small_kernel(
             leave_kernel, "leave_early", [scene_flag],
-            [normed_t, first[7], third[7], fourth[7], chip_cotangent, third[1], fourth[1],
+            [normed_t, first[7], third[7], fourth[7], gate(chip_cotangent, to_x, to_y), third[1], fourth[1],
              left_0, right_0, from_x0, from_y0],
             [((3 * quarter, half), BF)] * 2
             + [((quarter, half), F32)] * 2
@@ -672,18 +679,12 @@
             [pltpu.VMEM((4, PAIR, rows), BF)],
         )
         early_x, early_y = square(to_x, 1), square(to_y, 2)
-        rims_1 = lax.optimization_barrier((*rims_1, to_x, to_y))[:2]
-
-    if fast:
-        key_1, value_1, to_x, to_y = small_kernel(
-            rim_kernel, "rims_second", [even_flag],
-            [normed_t, *rims_1, third[2], fourth[2], third[3], fourth[3]],
-            [((rows, query_width), BF)] * 2 + [((model_width // 2, query_width), BF)] * 2,
-        )
-        late_x, late_y = square(to_x, 1), square(to_y, 2)
-        early_x, early_y, att_0, att_1 = lax.optimization_barrier(
-            (early_x, early_y, att_0, att_1, to_x, to_y)
-        )[:4]
+
+        left_0, key_1, value_1 = lax.optimization_barrier((left_0, key_1, value_1, to_x, to_y))[:3]
+        grad_0 = jnp.concatenate([left_0, right_0], axis=1)
+        ngrad_part = dot(grad_0, weights_0, ((1,), (1,))) + dot(
+            jnp.concatenate([third[1], fourth[1], key_1, value_1], axis=1), weights_1, ((1,), (1,))
+        )
         height = model_width // 4
         kept_0, sent = groups_of(
             left + early_y[2 * height :].astype(F32), right + early_x[2 * height :].astype(F32), 0
@@ -695,19 +696,14 @@
             [((height, half + quarter), BF)] * 2 + [((height, half + quarter), F32)] * 2,
         )
         end_x, end_y = square(to_x, 1), square(to_y, 2)
-        left_0, key_1, scale_first, got_0 = lax.optimization_barrier(
-            (left_0, key_1, first[6], got_0, to_x, to_y)
-        )[:4]
-        grad_0 = jnp.concatenate([left_0, right_0], axis=1)
+        att_0, att_1, got_0 = lax.optimization_barrier((att_0, att_1, got_0, to_x, to_y))[:3]
     else:
         key_1, value_1 = key_value_grads(
             *[jnp.concatenate([third[i], fourth[i]], axis=1) for i in (2, 3)], rims_1
         )
-        scale_first = first[6]
+        grad_1 = jnp.concatenate([third[1], fourth[1], key_1, value_1], axis=1)
+        ngrad_part = dot(grad_0, weights_0, ((1,), (1,))) + dot(grad_1, weights_1, ((1,), (1,)))
     mixed_part = dot(att_0, out_rows(CHUNKS[0])) + dot(att_1, out_rows(CHUNKS[1]))
-    grad_1 = jnp.concatenate([third[1], fourth[1], key_1, value_1], axis=1)
-
-    ngrad_part = dot(grad_0, weights_0, ((1,), (1,))) + dot(grad_1, weights_1, ((1,), (1,)))
     mixed_mine = lax.dynamic_slice_in_dim(mixed_part, core * own_rows, own_rows, 0)
     mixed_theirs = lax.dynamic_slice_in_dim(mixed_part, (1 - core) * own_rows, own_rows, 0)
     mixed = (
@@ -741,7 +737,7 @@
 
     scale_parts = {}
     for pairs, sums in zip(
-        CHUNKS, (scale_first, jnp.concatenate([third[6], fourth[6]], axis=0))
+        CHUNKS, (first[6], jnp.concatenate([third[6], fourth[6]], axis=0))
     ):
         sums = jnp.sum(sums.reshape(2, 8, 2, PAIR), axis=(1, 3))
         for i, p in enumerate(pairs):
@@ -751,17 +747,22 @@
 
     if fast:
         small = jnp.concatenate([gain_grad, scale_grad, jnp.zeros((112,), F32)]).reshape(9, 128)
+        end_x, end_y, small = lax.optimization_barrier((end_x, end_y, small))
         small = small + square(small, 1)
-        small = small + square(small, 2)
         kept_0, sent = halves_of(kept_0 + got_0.astype(F32))
         got_0 = chips(sent, 2, n_vox)
         kept_1, sent = groups_of(left + end_y.astype(F32), right + end_x.astype(F32), 1)
         got_1 = chips(sent, 1, n_vox)
+        small = gate(small, sent)
+        small = small + square(small, 2)
         small = small + lax.ppermute(small, "vox", swap)
-        small = small + chips(small, 1, n_vox)
+        got_1, small, token_grad = lax.optimization_barrier((got_1, small, token_grad))
         kept_1, sent = halves_of(kept_1 + got_1.astype(F32))
         got_1 = chips(sent, 2, n_vox)
+        small = gate(small, sent)
+        small = small + chips(small, 1, n_vox)
         small = small + chips(small, 2, n_vox)
+        got_1, small, mixed = lax.optimization_barrier((got_1, small, mixed))
         small = small.reshape(-1)
         summed_gain, summed_scale = small[:model_width], small[model_width : model_width + HEADS]
         kept_1 = kept_1 + got_1.astype(F32)

time: 196 us -> 186 us (0.949)
  other arithmetic: 27.3 us -> 18.5 us
  starting transfers between devices: 36.5 us -> 40.5 us
  Pallas kernels: 33 us -> 29.5 us
  local copies, waits for them, and re-layouts: 31.1 us -> 28.6 us
    ppermute x6, waiting for transfers between devices: 19.9 us -> 9.71 us  [chips(): return lax.ppermute(value, 'vox', [(i, i ^ 2 * step) for i in range(n_vox)])]
    ppermute x6, starting transfers between devices: 3.43 us -> 10.2 us  [chips(): return lax.ppermute(value, 'vox', [(i, i ^ 2 * step) for i in range(n_vox)])]
    ppermute x16, waiting for transfers between devices: 32.3 us -> 38.2 us  [square(): return lax.ppermute(value, 'fsdp', [(i, i ^ step) for i in range(4)])]
    ppermute x3, waiting for transfers between devices: 4.81 us -> 8.25 us  [pairings(): lax.ppermute(first, 'vox', near_chips)]
    pallas_call x6, Pallas kernels: 8.94 us -> 6.23 us  [small_kernel(): pl.pallas_call(kernel, grid_spec=pltpu.PrefetchScalarGridSpec(num_scalar_...]
    reduce_sum x4, other arithmetic: 2.6 us -> 0.21 us  [on_device(): sums = jnp.sum(sums.reshape(2, 8, 2, PAIR), axis=(1, 3))]
    ppermute x3, starting transfers between devices: 4.73 us -> 2.67 us  [pairings(): lax.ppermute(second, 'vox', far_chips)]
    unnamed x135 -> x157, local copies, waits for them, and re-layouts: 20.2 us -> 21.1 us
  transfers between devices with their start and end apart: 36 -> 36, of which waited for: 12 -> 15; matrix products, arithmetic and copies ran while one was open for 22% -> 17% of each run, Pallas kernels for 9% -> 7%
where the time goes in v1:
time: 186 us; the launch traced here: 185 us
  waiting for transfers between devices  56.7 us (30%)
  starting transfers between devices  40.5 us (22%)
  Pallas kernels  29.5 us (16%)
  local copies, waits for them, and re-layouts  28.6 us (15%)
  other arithmetic  18.5 us (10%)
  matrix products  9.56 us (5%)
  between operations  1.88 us (1%)
    ppermute x16, waiting for transfers between devices, square(): return lax.ppermute(value, 'fsdp', [(i, i ^ step) for i in range(4)])  38.2 us
    pallas_call x3, Pallas kernels, attention(): pl.pallas_call(attention_kernel, grid_spec=pltpu.PrefetchScalarGridSpec(n...  23.3 us
    unnamed x157, local copies, waits for them, and re-layouts  21.1 us
    ppermute x16, starting transfers between devices, square(): return lax.ppermute(value, 'fsdp', [(i, i ^ step) for i in range(4)])  17.8 us
    ppermute x6, starting transfers between devices, chips(): return lax.ppermute(value, 'vox', [(i, i ^ 2 * step) for i in range(n_vox)])  10.2 us
    ppermute x6, waiting for transfers between devices, chips(): return lax.ppermute(value, 'vox', [(i, i ^ 2 * step) for i in range(n_vox)])  9.71 us
    dot_general x7, matrix products, dot(): return lax.dot_general(a, b, (dims, ((), ())), preferred_element_type=F32)  9.56 us
    ppermute x3, waiting for transfers between devices, pairings(): lax.ppermute(first, 'vox', near_chips)  8.25 us
  transfers between devices with their start and end apart: 36, of which 15 were waited for; matrix products, arithmetic and copies ran while one was open for 17% of the time, Pallas kernels for 7%

profile of v1, /device:TPU:0, one launch (start us, length us, event | category | flops | bytes accessed | tf_op | source)
XLA Modules:
  0.0 185.3 jit_solution(12841378433870312886)
XLA Ops:
  5.7 2.6 %collective-permute-start.2 = (bf16[128,2048]{1,0:T(8,128)(2,1)S(1)}, bf16[128,2048]{1,0:T(8,128)(2,1)}, u32[]{:S(2)}, u32[]{:S(2)}) collective-permute-start(bf16[128,2048]{1,0:T(8,128)(2,1)S(1)} %get-tuple-element.77), channel_id=1, source_target_pairs={{0,2},{1,3},{2,0},{3,1},{4,6},{5,7},{6,4},{7,5},{8,10},{9,11},{10,... | collective-permute-start | bytes 1572872 | tf_op jit(solution)/shard_map/ppermute | solution.py:472
  8.3 1.5 collective-permute-start.3
  11.1 10.0 %collective-permute-done.2 = bf16[128,2048]{1,0:T(8,128)(2,1)} collective-permute-done((bf16[128,2048]{1,0:T(8,128)(2,1)S(1)}, bf16[128,2048]{1,0:T(8,128)(2,1)}, u32[]{:S(2)}, u32[]{:S(2)}) %collective-permute-start.2) | collective-permute-done | bytes 524320 | tf_op jit(solution)/shard_map/ppermute | solution.py:472
  21.0 1.5 collective-permute-done.3
  22.5 1.5 collective-permute-start.4
  27.6 1.7 collective-permute-start.6
  34.8 2.6 %collective-permute-done.4 = bf16[128,2048]{1,0:T(8,128)(2,1)S(1)} collective-permute-done((bf16[128,2048]{1,0:T(8,128)(2,1)S(1)}, bf16[128,2048]{1,0:T(8,128)(2,1)S(1)}, u32[]{:S(2)}, u32[]{:S(2)}) %collective-permute-start.4) | collective-permute-done | bytes 524320 | tf_op jit(solution)/shard_map/ppermute | solution.py:472
  38.4 8.5 %collective-permute-done.5 = bf16[128,2048]{1,0:T(8,128)(2,1)S(1)} collective-permute-done((bf16[128,2048]{1,0:T(8,128)(2,1)}, bf16[128,2048]{1,0:T(8,128)(2,1)S(1)}, u32[]{:S(2)}, u32[]{:S(2)}) %collective-permute-start.5) | collective-permute-done | bytes 524320 | tf_op jit(solution)/shard_map/ppermute | solution.py:472
  53.5 4.4 %collective-permute-start.8 = (bf16[192,1024]{1,0:T(8,128)(2,1)S(1)}, bf16[192,1024]{1,0:T(8,128)(2,1)S(1)}, u32[]{:S(2)}, u32[]{:S(2)}) collective-permute-start(bf16[192,1024]{1,0:T(8,128)(2,1)S(1)} %get-tuple-element.173), channel_id=1, source_target_pairs={{0,8},{4,12},{8,0},{12,4},{16,24},{20,28},{24,16},{28,20},{1,9},{5... | collective-permute-start | bytes 1179656 | tf_op jit(solution)/shard_map/ppermute | solution.py:588
  59.5 5.6 %collective-permute-done.8.k1_ref.v1_ref = bf16[192,1024]{1,0:T(8,128)(2,1)S(1)} collective-permute-done((bf16[192,1024]{1,0:T(8,128)(2,1)S(1)}, bf16[192,1024]{1,0:T(8,128)(2,1)S(1)}, u32[]{:S(2)}, u32[]{:S(2)}) %collective-permute-start.8) | collective-permute-done | bytes 393248 | tf_op jit(solution)/shard_map/ppermute | solution.py:588
  65.2 11.8 %block_attention.3 = (bf16[768,256]{1,0:T(8,128)(2,1)S(1)}, bf16[768,256]{1,0:T(8,128)(2,1)S(1)}, f32[768,256]{1,0:T(8,128)S(1)}, f32[768,256]{1,0:T(8,128)S(1)}...) custom-call(s32[12,8]{1,0:T(8,128)S(1)} %copy.24.mult_ref, ...), custom_call_target="tpu_custom_call" | custom-call | flops 19327352832 | bytes 3932160 | tf_op jit(solution)/shard_map/block_attention/pallas_call | solution.py:216
  77.5 1.7 collective-permute-start.11
  80.2 5.7 %block_attention.4 = (bf16[768,128]{1,0:T(8,128)(2,1)S(1)}, bf16[768,128]{1,0:T(8,128)(2,1)S(1)}, f32[768,128]{1,0:T(8,128)S(1)}, f32[768,128]{1,0:T(8,128)S(1)}...) custom-call(s32[12,8]{1,0:T(8,128)S(1)} %copy.24.mult_ref, ...), custom_call_target="tpu_custom_call" | custom-call | flops 9663676416 | bytes 1966080 | tf_op jit(solution)/shard_map/block_attention/pallas_call | solution.py:216
  88.4 5.8 %block_attention.5 = (bf16[768,256]{1,0:T(8,128)(2,1)S(1)}, bf16[768,128]{1,0:T(8,128)(2,1)S(1)}, f32[768,128]{1,0:T(8,128)S(1)}, f32[768,128]{1,0:T(8,128)S(1)}...) custom-call(s32[12,8]{1,0:T(8,128)S(1)} %copy.24.mult_ref, ...), custom_call_target="tpu_custom_call" | custom-call | flops 9663676416 | bytes 1966080 | tf_op jit(solution)/shard_map/block_attention/pallas_call | solution.py:216
  94.2 2.0 %collective-permute-start.13 = (bf16[2,192,256]{2,1,0:T(8,128)(2,1)S(1)}, bf16[2,192,256]{2,1,0:T(8,128)(2,1)S(1)}, u32[]{:S(2)}, u32[]{:S(2)}) collective-permute-start(bf16[2,192,256]{2,1,0:T(8,128)(2,1)S(1)} %get-tuple-element.97), channel_id=1, source_target_pairs={{0,8},{4,12},{8,0},{12,4},{16,24},{20,28},{24,16},{28,20},{1,9},{5... | collective-permute-start | bytes 589832 | tf_op jit(solution)/shard_map/ppermute | solution.py:588
  97.3 2.6 %collective-permute-done.13.refs_1_ = bf16[2,192,256]{2,1,0:T(8,128)(2,1)S(1)} collective-permute-done((bf16[2,192,256]{2,1,0:T(8,128)(2,1)S(1)}, bf16[2,192,256]{2,1,0:T(8,128)(2,1)S(1)}, u32[]{:S(2)}, u32[]{:S(2)}) %collective-permute-start.13) | collective-permute-done | bytes 196640 | tf_op jit(solution)/shard_map/ppermute | solution.py:588
  103.5 2.8 %leave_early.1 = (bf16[768,384]{1,0:T(8,128)(2,1)}, bf16[768,384]{1,0:T(8,128)(2,1)S(1)}, f32[256,384]{1,0:T(8,128)S(1)}, f32[256,384]{1,0:T(8,128)S(1)}, f32[2,...) custom-call(s32[1]{0:T(128)} %bitcast.9.scene_ref, bf16[1024,768]{1,0:T(8,128)(2,1)S(1)} %turn.1.refs_0_.t_ref, ...), custom_call_target="tpu_custom_call" | custom-call | tf_op jit(solution)/shard_map/leave_early/pallas_call | solution.py:303
  110.2 1.4 collective-permute-start.17
  115.7 3.2 %fusion.17 = f32[768,1024]{1,0:T(8,128)S(1)} fusion(bf16[1024,768]{1,0:T(8,128)(2,1)} %copy-done.73, bf16[768,256]{1,0:T(8,128)(2,1)} %copy-done.22, bf16[768,256]{1,0:T(8,128)(2,1)} %copy-done.20, bf16[768,128]{1,0:T(8,128)(2,1)} %copy-done.3, bf16[768,128]{1,0:T(8,128)(2,1)S(1)} %get-tuple-element.82.q1_ref), kind=kOutput, calls=%fused_computation.35 | convolution fusion | flops 1212678144 | bytes 5898240 | tf_op jit(solution)/shard_map/dot_general | solution.py:22
  118.9 5.2 %collective-permute-done.17.ex_ref = bf16[768,384]{1,0:T(8,128)(2,1)S(1)} collective-permute-done((bf16[768,384]{1,0:T(8,128)(2,1)}, bf16[768,384]{1,0:T(8,128)(2,1)S(1)}, u32[]{:S(2)}, u32[]{:S(2)}) %collective-permute-start.17) | collective-permute-done | bytes 589856 | tf_op jit(solution)/shard_map/ppermute | solution.py:472
  124.2 5.6 %collective-permute-done.18.ey_ref = bf16[768,384]{1,0:T(8,128)(2,1)S(1)} collective-permute-done((bf16[768,384]{1,0:T(8,128)(2,1)}, bf16[768,384]{1,0:T(8,128)(2,1)S(1)}, u32[]{:S(2)}, u32[]{:S(2)}) %collective-permute-start.18) | collective-permute-done | bytes 589856 | tf_op jit(solution)/shard_map/ppermute | solution.py:472
  130.6 3.4 %collective-permute-start.31 = (bf16[256,384]{1,0:T(8,128)(2,1)S(1)}, bf16[256,384]{1,0:T(8,128)(2,1)S(1)}, u32[]{:S(2)}, u32[]{:S(2)}) collective-permute-start(bf16[256,384]{1,0:T(8,128)(2,1)S(1)} %select_convert_fusion.1), channel_id=1, source_target_pairs={{0,8},{4,12},{8,0},{12,4},{16,24},{20,28},{24,16},{28,20},{1,9},{5... | collective-permute-start | bytes 589832 | tf_op jit(solution)/shard_map/ppermute | solution.py:476
  148.8 2.2 %dynamic-slice_add_fusion = f32[384,1024]{1,0:T(8,128)S(1)} fusion(f32[384,1024]{1,0:T(8,128)} %collective-permute-done.23, f32[768,1024]{1,0:T(8,128)} %copy-done.35, s32[]{:T(128)S(6)} %select_n.459), kind=kLoop, calls=%fused_computation.28 | loop fusion | flops 393216 | bytes 4718596 | tf_op jit(solution)/shard_map/add | solution.py:715
  151.3 2.2 %copy-done.37 = f32[768,1024]{1,0:T(8,128)S(1)} copy-done((f32[768,1024]{1,0:T(8,128)S(1)}, f32[768,1024]{1,0:T(8,128)}, u32[]{:S(2)}) %copy-start.37) | copy-done | bytes 3145752
  153.5 2.9 %fusion.12 = (f32[384]{0:T(512)S(1)}, f32[1024]{0:T(1024)S(1)}, bf16[384,1024]{1,0:T(8,128)(2,1)}) fusion(f32[1024]{0:T(1024)S(1)} %copy-done.71, f32[384,256]{1,0:T(8,128)S(1)} %get-tuple-element.154, f32[384,256]{1,0:T(8,128)S(1)} %get-tuple-element.153, f32[384,256]{1,0:T(8,128)S(1)} %get-tuple-element.152, f32[384,256]{1,0:T(8,128)S(1)} %get-tuple-element.151, ...), kind=kLoop, calls=%fused_computation.22 | loop fusion | flops 5110400 | bytes 6302724 | tf_op jit(solution)/shard_map/reduce_sum | solution.py:734
  158.6 2.1 %collective-permute-start.24 = (bf16[256,640]{1,0:T(8,128)(2,1)S(1)}, bf16[256,640]{1,0:T(8,128)(2,1)S(1)}, u32[]{:S(2)}, u32[]{:S(2)}) collective-permute-start(bf16[256,640]{1,0:T(8,128)(2,1)S(1)} %select_convert_fusion), channel_id=1, source_target_pairs={{0,8},{4,12},{8,0},{12,4},{16,24},{20,28},{24,16},{28,20},{1,9},{5... | collective-permute-start | bytes 983048 | tf_op jit(solution)/shard_map/ppermute | solution.py:476
  162.3 2.9 %collective-permute-done.26 = f32[9,128]{1,0:T(8,128)S(1)} collective-permute-done((f32[9,128]{1,0:T(8,128)S(1)}, f32[9,128]{1,0:T(8,128)S(1)}, u32[]{:S(2)}, u32[]{:S(2)}) %collective-permute-start.26) | collective-permute-done | bytes 4640 | tf_op jit(solution)/shard_map/ppermute | solution.py:472
  165.3 1.5 fusion.11
  168.2 1.8 collective-permute-start.29
  170.3 1.6 collective-permute-done.29
  172.0 1.6 collective-permute-start.30
  174.5 6.8 %collective-permute-done.30 = f32[9,128]{1,0:T(8,128)S(1)} collective-permute-done((f32[9,128]{1,0:T(8,128)S(1)}, f32[9,128]{1,0:T(8,128)S(1)}, u32[]{:S(2)}, u32[]{:S(2)}) %collective-permute-start.30) | collective-permute-done | bytes 4640 | tf_op jit(solution)/shard_map/ppermute | solution.py:476
  (304 shorter events, 66.8 us)
Async XLA Ops:
  2.1 8.7 %collective-permute-start.1 = (f32[6,9]{0,1:T(8,128)S(1)}, f32[6,9]{0,1:T(8,128)S(1)}, u32[]{:S(2)}, u32[]{:S(2)}) collective-permute-start(f32[6,9]{0,1:T(8,128)S(1)} %fusion.43), channel_id=1, source_target_pairs={{0,4},{4,0},{8,12},{12,8},{16,20},{20,16},{24,28},{28,24},{1,5},{5... | collective-permute-start | bytes 656 | tf_op jit(solution)/shard_map/ppermute | solution.py:557
  2.5 24.2 %collective-permute-start = (bf16[384,1024]{1,0:T(8,128)(2,1)}, bf16[384,1024]{1,0:T(8,128)(2,1)S(1)}, u32[]{:S(2)}, u32[]{:S(2)}) collective-permute-start(bf16[384,1024]{1,0:T(8,128)(2,1)} %bitcast.51), channel_id=1, source_target_pairs={{0,4},{4,0},{8,12},{12,8},{16,20},{20,16},{24,28},{28,24},{1,5},{5... | collective-permute-start | bytes 2359304 | tf_op jit(solution)/shard_map/ppermute | solution.py:553
  2.6 29.2 %collective-permute-start.10 = (bf16[384,1024]{1,0:T(8,128)(2,1)}, bf16[384,1024]{1,0:T(8,128)(2,1)}, u32[]{:S(2)}, u32[]{:S(2)}) collective-permute-start(bf16[384,1024]{1,0:T(8,128)(2,1)} %bitcast.52), channel_id=1, source_target_pairs={{0,4},{4,0},{8,12},{12,8},{16,20},{20,16},{24,28},{28,24},{1,5},{5... | collective-permute-start | bytes 2359304 | tf_op jit(solution)/shard_map/ppermute | solution.py:554
  5.7 15.3 %collective-permute-start.2 = (bf16[128,2048]{1,0:T(8,128)(2,1)S(1)}, bf16[128,2048]{1,0:T(8,128)(2,1)}, u32[]{:S(2)}, u32[]{:S(2)}) collective-permute-start(bf16[128,2048]{1,0:T(8,128)(2,1)S(1)} %get-tuple-element.77), channel_id=1, source_target_pairs={{0,2},{1,3},{2,0},{3,1},{4,6},{5,7},{6,4},{7,5},{8,10},{9,11},{10,... | collective-permute-start | bytes 1572872 | tf_op jit(solution)/shard_map/ppermute | solution.py:472
  8.3 14.2 %collective-permute-start.3 = (bf16[128,2048]{1,0:T(8,128)(2,1)S(1)}, bf16[128,2048]{1,0:T(8,128)(2,1)}, u32[]{:S(2)}, u32[]{:S(2)}) collective-permute-start(bf16[128,2048]{1,0:T(8,128)(2,1)S(1)} %get-tuple-element.78), channel_id=1, source_target_pairs={{0,1},{1,0},{2,3},{3,2},{4,5},{5,4},{6,7},{7,6},{8,9},{9,8},{10,11... | collective-permute-start | bytes 1572872 | tf_op jit(solution)/shard_map/ppermute | solution.py:472
  22.5 14.9 %collective-permute-start.4 = (bf16[128,2048]{1,0:T(8,128)(2,1)S(1)}, bf16[128,2048]{1,0:T(8,128)(2,1)S(1)}, u32[]{:S(2)}, u32[]{:S(2)}) collective-permute-start(bf16[128,2048]{1,0:T(8,128)(2,1)S(1)} %get-tuple-element.77), channel_id=1, source_target_pairs={{0,1},{1,0},{2,3},{3,2},{4,5},{5,4},{6,7},{7,6},{8,9},{9,8},{10,11... | collective-permute-start | bytes 1572872 | tf_op jit(solution)/shard_map/ppermute | solution.py:472
  24.0 25.3 %collective-permute-start.7 = (bf16[128,2048]{1,0:T(8,128)(2,1)S(1)}, bf16[128,2048]{1,0:T(8,128)(2,1)S(1)}, u32[]{:S(2)}, u32[]{:S(2)}) collective-permute-start(bf16[128,2048]{1,0:T(8,128)(2,1)S(1)} %get-tuple-element.78), channel_id=1, source_target_pairs={{0,2},{1,3},{2,0},{3,1},{4,6},{5,7},{6,4},{7,5},{8,10},{9,11},{10,... | collective-permute-start | bytes 1572872 | tf_op jit(solution)/shard_map/ppermute | solution.py:472
  25.4 21.5 %collective-permute-start.5 = (bf16[128,2048]{1,0:T(8,128)(2,1)}, bf16[128,2048]{1,0:T(8,128)(2,1)S(1)}, u32[]{:S(2)}, u32[]{:S(2)}) collective-permute-start(bf16[128,2048]{1,0:T(8,128)(2,1)} %collective-permute-done.2), channel_id=1, source_target_pairs={{0,1},{1,0},{2,3},{3,2},{4,5},{5,4},{6,7},{7,6},{8,9},{9,8},{10,11... | collective-permute-start | bytes 1572872 | tf_op jit(solution)/shard_map/ppermute | solution.py:472
  27.6 20.5 %collective-permute-start.6 = (bf16[128,2048]{1,0:T(8,128)(2,1)}, bf16[128,2048]{1,0:T(8,128)(2,1)S(1)}, u32[]{:S(2)}, u32[]{:S(2)}) collective-permute-start(bf16[128,2048]{1,0:T(8,128)(2,1)} %collective-permute-done.3), channel_id=1, source_target_pairs={{0,2},{1,3},{2,0},{3,1},{4,6},{5,7},{6,4},{7,5},{8,10},{9,11},{10,... | collective-permute-start | bytes 1572872 | tf_op jit(solution)/shard_map/ppermute | solution.py:472
  52.6 6.9 %collective-permute-start.9 = (bf16[192,1024]{1,0:T(8,128)(2,1)S(1)}, bf16[192,1024]{1,0:T(8,128)(2,1)S(1)}, u32[]{:S(2)}, u32[]{:S(2)}) collective-permute-start(bf16[192,1024]{1,0:T(8,128)(2,1)S(1)} %get-tuple-element.172), channel_id=1, source_target_pairs={{0,0},{4,4},{8,16},{12,20},{16,8},{20,12},{24,24},{28,28},{1,1},{5... | collective-permute-start | bytes 1179656 | tf_op jit(solution)/shard_map/ppermute | solution.py:588
  53.5 11.6 %collective-permute-start.8 = (bf16[192,1024]{1,0:T(8,128)(2,1)S(1)}, bf16[192,1024]{1,0:T(8,128)(2,1)S(1)}, u32[]{:S(2)}, u32[]{:S(2)}) collective-permute-start(bf16[192,1024]{1,0:T(8,128)(2,1)S(1)} %get-tuple-element.173), channel_id=1, source_target_pairs={{0,8},{4,12},{8,0},{12,4},{16,24},{20,28},{24,16},{28,20},{1,9},{5... | collective-permute-start | bytes 1179656 | tf_op jit(solution)/shard_map/ppermute | solution.py:588
  77.5 8.4 %collective-permute-start.11 = (bf16[2,192,256]{2,1,0:T(8,128)(2,1)S(1)}, bf16[2,192,256]{2,1,0:T(8,128)(2,1)S(1)}, u32[]{:S(2)}, u32[]{:S(2)}) collective-permute-start(bf16[2,192,256]{2,1,0:T(8,128)(2,1)S(1)} %get-tuple-element.79), channel_id=1, source_target_pairs={{0,8},{4,12},{8,0},{12,4},{16,24},{20,28},{24,16},{28,20},{1,9},{5... | collective-permute-start | bytes 589832 | tf_op jit(solution)/shard_map/ppermute | solution.py:588
  79.3 6.6 %collective-permute-start.12 = (bf16[2,192,256]{2,1,0:T(8,128)(2,1)S(1)}, bf16[2,192,256]{2,1,0:T(8,128)(2,1)S(1)}, u32[]{:S(2)}, u32[]{:S(2)}) collective-permute-start(bf16[2,192,256]{2,1,0:T(8,128)(2,1)S(1)} %get-tuple-element.80), channel_id=1, source_target_pairs={{0,0},{4,4},{8,16},{12,20},{16,8},{20,12},{24,24},{28,28},{1,1},{5... | collective-permute-start | bytes 589832 | tf_op jit(solution)/shard_map/ppermute | solution.py:588
  87.0 16.5 %collective-permute-start.15 = (bf16[512,384]{1,0:T(8,128)(2,1)S(1)}, bf16[512,384]{1,0:T(8,128)(2,1)S(1)}, u32[]{:S(2)}, u32[]{:S(2)}) collective-permute-start(bf16[512,384]{1,0:T(8,128)(2,1)S(1)} %get-tuple-element.89), channel_id=1, source_target_pairs={{0,1},{1,0},{2,3},{3,2},{4,5},{5,4},{6,7},{7,6},{8,9},{9,8},{10,11... | collective-permute-start | bytes 1179656 | tf_op jit(solution)/shard_map/ppermute | solution.py:472
  87.7 15.8 %collective-permute-start.16 = (bf16[512,384]{1,0:T(8,128)(2,1)S(1)}, bf16[512,384]{1,0:T(8,128)(2,1)S(1)}, u32[]{:S(2)}, u32[]{:S(2)}) collective-permute-start(bf16[512,384]{1,0:T(8,128)(2,1)S(1)} %get-tuple-element.90), channel_id=1, source_target_pairs={{0,2},{1,3},{2,0},{3,1},{4,6},{5,7},{6,4},{7,5},{8,10},{9,11},{10,... | collective-permute-start | bytes 1179656 | tf_op jit(solution)/shard_map/ppermute | solution.py:472
  94.2 5.7 %collective-permute-start.13 = (bf16[2,192,256]{2,1,0:T(8,128)(2,1)S(1)}, bf16[2,192,256]{2,1,0:T(8,128)(2,1)S(1)}, u32[]{:S(2)}, u32[]{:S(2)}) collective-permute-start(bf16[2,192,256]{2,1,0:T(8,128)(2,1)S(1)} %get-tuple-element.97), channel_id=1, source_target_pairs={{0,8},{4,12},{8,0},{12,4},{16,24},{20,28},{24,16},{28,20},{1,9},{5... | collective-permute-start | bytes 589832 | tf_op jit(solution)/shard_map/ppermute | solution.py:588
  96.2 3.7 %collective-permute-start.14 = (bf16[2,192,256]{2,1,0:T(8,128)(2,1)S(1)}, bf16[2,192,256]{2,1,0:T(8,128)(2,1)S(1)}, u32[]{:S(2)}, u32[]{:S(2)}) collective-permute-start(bf16[2,192,256]{2,1,0:T(8,128)(2,1)S(1)} %get-tuple-element.98), channel_id=1, source_target_pairs={{0,0},{4,4},{8,16},{12,20},{16,8},{20,12},{24,24},{28,28},{1,1},{5... | collective-permute-start | bytes 589832 | tf_op jit(solution)/shard_map/ppermute | solution.py:588
  110.2 13.9 %collective-permute-start.17 = (bf16[768,384]{1,0:T(8,128)(2,1)}, bf16[768,384]{1,0:T(8,128)(2,1)S(1)}, u32[]{:S(2)}, u32[]{:S(2)}) collective-permute-start(bf16[768,384]{1,0:T(8,128)(2,1)} %get-tuple-element.112), channel_id=1, source_target_pairs={{0,1},{1,0},{2,3},{3,2},{4,5},{5,4},{6,7},{7,6},{8,9},{9,8},{10,11... | collective-permute-start | bytes 1769480 | tf_op jit(solution)/shard_map/ppermute | solution.py:472
  113.0 24.8 %collective-permute-start.19 = (bf16[512,256]{1,0:T(8,128)(2,1)}, bf16[512,256]{1,0:T(8,128)(2,1)S(1)}, u32[]{:S(2)}, u32[]{:S(2)}) collective-permute-start(bf16[512,256]{1,0:T(8,128)(2,1)} %copy-done.34), channel_id=1, source_target_pairs={{0,1},{1,0},{2,3},{3,2},{4,5},{5,4},{6,7},{7,6},{8,9},{9,8},{10,11... | collective-permute-start | bytes 786440 | tf_op jit(solution)/shard_map/ppermute | solution.py:472
  113.7 24.1 %collective-permute-start.20 = (bf16[512,256]{1,0:T(8,128)(2,1)}, bf16[512,256]{1,0:T(8,128)(2,1)S(1)}, u32[]{:S(2)}, u32[]{:S(2)}) collective-permute-start(bf16[512,256]{1,0:T(8,128)(2,1)} %copy-done.33), channel_id=1, source_target_pairs={{0,2},{1,3},{2,0},{3,1},{4,6},{5,7},{6,4},{7,5},{8,10},{9,11},{10,... | collective-permute-start | bytes 786440 | tf_op jit(solution)/shard_map/ppermute | solution.py:472
  115.0 14.8 %collective-permute-start.18 = (bf16[768,384]{1,0:T(8,128)(2,1)}, bf16[768,384]{1,0:T(8,128)(2,1)S(1)}, u32[]{:S(2)}, u32[]{:S(2)}) collective-permute-start(bf16[768,384]{1,0:T(8,128)(2,1)} %copy-done.28), channel_id=1, source_target_pairs={{0,2},{1,3},{2,0},{3,1},{4,6},{5,7},{6,4},{7,5},{8,10},{9,11},{10,... | collective-permute-start | bytes 1769480 | tf_op jit(solution)/shard_map/ppermute | solution.py:472
  130.6 9.0 %collective-permute-start.31 = (bf16[256,384]{1,0:T(8,128)(2,1)S(1)}, bf16[256,384]{1,0:T(8,128)(2,1)S(1)}, u32[]{:S(2)}, u32[]{:S(2)}) collective-permute-start(bf16[256,384]{1,0:T(8,128)(2,1)S(1)} %select_convert_fusion.1), channel_id=1, source_target_pairs={{0,8},{4,12},{8,0},{12,4},{16,24},{20,28},{24,16},{28,20},{1,9},{5... | collective-permute-start | bytes 589832 | tf_op jit(solution)/shard_map/ppermute | solution.py:476
  137.8 11.0 %collective-permute-start.23 = (f32[384,1024]{1,0:T(8,128)}, f32[384,1024]{1,0:T(8,128)}, u32[]{:S(2)}, u32[]{:S(2)}) collective-permute-start(f32[384,1024]{1,0:T(8,128)} %constant_dynamic-slice_fusion.1), channel_id=1, source_target_pairs={{0,4},{4,0},{8,12},{12,8},{16,20},{20,16},{24,28},{28,24},{1,5},{5... | collective-permute-start | bytes 4718600 | tf_op jit(solution)/shard_map/ppermute | solution.py:715
  144.1 7.2 %collective-permute-start.32 = (f32[384,1024]{1,0:T(8,128)}, f32[384,1024]{1,0:T(8,128)}, u32[]{:S(2)}, u32[]{:S(2)}) collective-permute-start(f32[384,1024]{1,0:T(8,128)} %constant_dynamic-slice_fusion), channel_id=1, source_target_pairs={{0,4},{4,0},{8,12},{12,8},{16,20},{20,16},{24,28},{28,24},{1,5},{5... | collective-permute-start | bytes 4718600 | tf_op jit(solution)/shard_map/ppermute | solution.py:710
  144.4 12.1 %collective-permute-start.21 = (bf16[256,640]{1,0:T(8,128)(2,1)S(1)}, bf16[256,640]{1,0:T(8,128)(2,1)}, u32[]{:S(2)}, u32[]{:S(2)}) collective-permute-start(bf16[256,640]{1,0:T(8,128)(2,1)S(1)} %copy-done.32), channel_id=1, source_target_pairs={{0,1},{1,0},{2,3},{3,2},{4,5},{5,4},{6,7},{7,6},{8,9},{9,8},{10,11... | collective-permute-start | bytes 983048 | tf_op jit(solution)/shard_map/ppermute | solution.py:472
  145.8 10.7 %collective-permute-start.22 = (bf16[256,640]{1,0:T(8,128)(2,1)S(1)}, bf16[256,640]{1,0:T(8,128)(2,1)S(1)}, u32[]{:S(2)}, u32[]{:S(2)}) collective-permute-start(bf16[256,640]{1,0:T(8,128)(2,1)S(1)} %copy-done.30), channel_id=1, source_target_pairs={{0,2},{1,3},{2,0},{3,1},{4,6},{5,7},{6,4},{7,5},{8,10},{9,11},{10,... | collective-permute-start | bytes 983048 | tf_op jit(solution)/shard_map/ppermute | solution.py:472
  147.8 25.8 %collective-permute-start.33 = (bf16[256,256]{1,0:T(8,128)(2,1)}, bf16[256,256]{1,0:T(8,128)(2,1)}, u32[]{:S(2)}, u32[]{:S(2)}) collective-permute-start(bf16[256,256]{1,0:T(8,128)(2,1)} %select_convert_fusion.3), channel_id=1, source_target_pairs={{0,16},{4,20},{8,24},{12,28},{16,0},{20,4},{24,8},{28,12},{1,17},{... | collective-permute-start | bytes 393224 | tf_op jit(solution)/shard_map/ppermute | solution.py:476
  157.8 3.7 %collective-permute-start.25 = (f32[9,128]{1,0:T(8,128)S(1)}, f32[9,128]{1,0:T(8,128)S(1)}, u32[]{:S(2)}, u32[]{:S(2)}) collective-permute-start(f32[9,128]{1,0:T(8,128)S(1)} %bitcast.57), channel_id=1, source_target_pairs={{0,1},{1,0},{2,3},{3,2},{4,5},{5,4},{6,7},{7,6},{8,9},{9,8},{10,11... | collective-permute-start | bytes 13832 | tf_op jit(solution)/shard_map/ppermute | solution.py:472
  158.6 9.4 %collective-permute-start.24 = (bf16[256,640]{1,0:T(8,128)(2,1)S(1)}, bf16[256,640]{1,0:T(8,128)(2,1)S(1)}, u32[]{:S(2)}, u32[]{:S(2)}) collective-permute-start(bf16[256,640]{1,0:T(8,128)(2,1)S(1)} %select_convert_fusion), channel_id=1, source_target_pairs={{0,8},{4,12},{8,0},{12,4},{16,24},{20,28},{24,16},{28,20},{1,9},{5... | collective-permute-start | bytes 983048 | tf_op jit(solution)/shard_map/ppermute | solution.py:476
  168.2 3.7 %collective-permute-start.29 = (f32[9,128]{1,0:T(8,128)S(1)}, f32[9,128]{1,0:T(8,128)S(1)}, u32[]{:S(2)}, u32[]{:S(2)}) collective-permute-start(f32[9,128]{1,0:T(8,128)S(1)} %add.163), channel_id=1, source_target_pairs={{0,8},{4,12},{8,0},{12,4},{16,24},{20,28},{24,16},{28,20},{1,9},{5... | collective-permute-start | bytes 13832 | tf_op jit(solution)/shard_map/ppermute | solution.py:476
  170.0 11.3 %collective-permute-start.28 = (bf16[384,256]{1,0:T(8,128)(2,1)S(1)}, bf16[384,256]{1,0:T(8,128)(2,1)S(1)}, u32[]{:S(2)}, u32[]{:S(2)}) collective-permute-start(bf16[384,256]{1,0:T(8,128)(2,1)S(1)} %select_convert_fusion.2), channel_id=1, source_target_pairs={{0,16},{4,20},{8,24},{12,28},{16,0},{20,4},{24,8},{28,12},{1,17},{... | collective-permute-start | bytes 589832 | tf_op jit(solution)/shard_map/ppermute | solution.py:476
  172.0 9.4 %collective-permute-start.30 = (f32[9,128]{1,0:T(8,128)S(1)}, f32[9,128]{1,0:T(8,128)S(1)}, u32[]{:S(2)}, u32[]{:S(2)}) collective-permute-start(f32[9,128]{1,0:T(8,128)S(1)} %add.166), channel_id=1, source_target_pairs={{0,16},{4,20},{8,24},{12,28},{16,0},{20,4},{24,8},{28,12},{1,17},{... | collective-permute-start | bytes 13832 | tf_op jit(solution)/shard_map/ppermute | solution.py:476
  (79 other events, 277.5 us)

commit v2 on v1

--- a/solution.py
+++ b/solution.py
@@ -330,99 +330,116 @@
             turned_ref[j : j + PAIR, i : i + PAIR] = jnp.transpose(tile).astype(BF)
 
 
-def rim_kernel(even_ref, *refs):
-    t_ref, rim1_ref, rim2_ref = refs[:3]
+def with_returned(even, rim1_ref, rim2_ref, index, grad):
+    margin, rows = rim1_ref.shape[1], grad.shape[0]
+    one, two = rim1_ref[index].astype(F32), rim2_ref[index].astype(F32)
+    return jnp.concatenate(
+        [
+            grad[:margin] + jnp.where(even, two, one),
+            grad[margin : rows - margin],
+            grad[rows - margin :] + jnp.where(even, one, two),
+        ],
+        axis=0,
+    ).astype(BF)
+
+
+def first_kernel(
+    even_ref, t_ref, rim1_ref, rim2_ref, q_ref, dk_ref, dv_ref, left_ref, right_ref, x_ref, y_ref
+):
     even = even_ref[0] == 1
-    margin = rim1_ref.shape[1]
     size = t_ref.shape[0] // 4
-
-    def added(index, grad):
-        rows = grad.shape[0]
-        one, two = rim1_ref[index].astype(F32), rim2_ref[index].astype(F32)
-        return jnp.concatenate(
-            [
-                grad[:margin] + jnp.where(even, two, one),
-                grad[margin : rows - margin],
-                grad[rows - margin :] + jnp.where(even, one, two),
-            ],
-            axis=0,
-        ).astype(BF)
-
-    if len(refs) == 10:
-        q_ref, dk_ref, dv_ref, left_ref, right_ref, x_ref, y_ref = refs[3:]
-        keys, values = added(0, dk_ref[...]), added(1, dv_ref[...])
-        left_ref[:, : 2 * PAIR] = q_ref[...]
-        left_ref[:, 2 * PAIR :] = keys[:, :PAIR]
-        right_ref[:, :PAIR] = keys[:, PAIR:]
-        right_ref[:, PAIR:] = values
-    else:
-        ka_ref, kb_ref, va_ref, vb_ref, left_ref, right_ref, x_ref, y_ref = refs[3:]
-        left_ref[...] = added(0, jnp.concatenate([ka_ref[...], kb_ref[...]], axis=1))
-        right_ref[...] = added(1, jnp.concatenate([va_ref[...], vb_ref[...]], axis=1))
+    keys = with_returned(even, rim1_ref, rim2_ref, 0, dk_ref[...])
+    left_ref[:, : 2 * PAIR] = q_ref[...]
+    left_ref[:, 2 * PAIR :] = keys[:, :PAIR]
+    right_ref[:, :PAIR] = keys[:, PAIR:]
+    right_ref[:, PAIR:] = with_returned(even, rim1_ref, rim2_ref, 1, dv_ref[...])
     x_ref[...] = dot(t_ref[: 2 * size, :], left_ref[...]).astype(BF)
     y_ref[...] = dot(t_ref[size : 3 * size, :], right_ref[...]).astype(BF)
 
 
+def put_tiles(ref, at, stride, value):
+    height = value.shape[0]
+    for j in range(value.shape[1] // PAIR):
+        start = at + j * stride
+        ref[start : start + height, :] = value[:, j * PAIR : (j + 1) * PAIR].astype(BF)
+
+
+def get_tiles(ref, at, stride, height, count):
+    return jnp.concatenate(
+        [ref[at + j * stride : at + j * stride + height, :].astype(F32) for j in range(count)],
+        axis=1,
+    )
+
+
 def leave_kernel(
-    scene_ref, t_ref, a0_ref, a1_ref, a2_ref, cot_ref, q1_ref, q2_ref, left_ref, right_ref, fx_ref, fy_ref,
-    x_ref, y_ref, kl_ref, kr_ref, e_ref, o_ref, at_ref,
+    scene_ref, even_ref, t_ref, rim1_ref, rim2_ref, ka_ref, kb_ref, va_ref, vb_ref,
+    a0_ref, a1_ref, a2_ref, cot_ref, q1_ref, q2_ref, left_ref, right_ref, fx_ref, fy_ref,
+    x_ref, y_ref, key_ref, value_ref, kept_ref, extra_ref, at_ref,
 ):
+    even = even_ref[0] == 1
     size = t_ref.shape[0] // 4
+    two = 2 * size
     quarter = cot_ref.shape[1] // 4
+    key_ref[...] = with_returned(
+        even, rim1_ref, rim2_ref, 0, jnp.concatenate([ka_ref[...], kb_ref[...]], axis=1)
+    )
+    value_ref[...] = with_returned(
+        even, rim1_ref, rim2_ref, 1, jnp.concatenate([va_ref[...], vb_ref[...]], axis=1)
+    )
+    to_x, to_y = t_ref[:two, :], t_ref[size : 3 * size, :]
+    put_tiles(x_ref, 0, two, dot(to_x, q1_ref[...]))
+    put_tiles(y_ref, 0, two, dot(to_y, q2_ref[...]))
+    put_tiles(x_ref, two, two, dot(to_x, key_ref[...]))
+    put_tiles(y_ref, two, two, dot(to_y, value_ref[...]))
     at_ref[0] = a0_ref[:PAIR, :]
     at_ref[3] = a0_ref[PAIR:, :]
     at_ref[1] = a1_ref[...]
     at_ref[2] = a2_ref[...]
-    x_ref[: 2 * size, :PAIR] = dot(t_ref[: 2 * size, :], q1_ref[...]).astype(BF)
-    y_ref[: 2 * size, :PAIR] = dot(t_ref[size : 3 * size, :], q2_ref[...]).astype(BF)
     for i, k in enumerate(ORDER):
         grad = dot(at_ref[jnp.bitwise_xor(scene_ref[0], k)], cot_ref[...])
-        evens = jnp.concatenate(
-            [grad[:, :quarter], grad[:, 2 * quarter : 3 * quarter]], axis=0
-        )
-        odds = jnp.concatenate(
-            [grad[:, quarter : 2 * quarter], grad[:, 3 * quarter :]], axis=0
-        )
+        evens = jnp.concatenate([grad[:, :quarter], grad[:, 2 * quarter : 3 * quarter]], axis=0)
+        odds = jnp.concatenate([grad[:, quarter : 2 * quarter], grad[:, 3 * quarter :]], axis=0)
         if i < 2:
-            x_ref[i * size : (i + 1) * size, PAIR:] = evens.astype(BF)
+            put_tiles(x_ref, 3 * two + i * size, two, evens)
         else:
-            e_ref[i - 2] = evens
+            extra_ref[i - 2] = evens
         if i in (1, 2):
-            y_ref[(i - 1) * size : i * size, PAIR:] = odds.astype(BF)
+            put_tiles(y_ref, 3 * two + (i - 1) * size, two, odds)
         else:
-            o_ref[i // 3] = odds
+            extra_ref[2 + i // 3] = odds
     left, right = left_ref[...], right_ref[...]
-    y_ref[2 * size :, :] = (
-        dot(t_ref[2 * size : 3 * size, :], left) + fx_ref[size:, :].astype(F32)
-    ).astype(BF)
-    x_ref[2 * size :, :] = (dot(t_ref[:size, :], right) + fy_ref[:size, :].astype(F32)).astype(BF)
-    kl_ref[...] = dot(t_ref[3 * size :, :], left) + fx_ref[:size, :].astype(F32)
-    kr_ref[...] = dot(t_ref[3 * size :, :], right) + fy_ref[size:, :].astype(F32)
+    put_tiles(
+        y_ref, 5 * two, size, dot(t_ref[two : 3 * size, :], left) + fx_ref[size:, :].astype(F32)
+    )
+    put_tiles(x_ref, 5 * two, size, dot(t_ref[:size, :], right) + fy_ref[:size, :].astype(F32))
+    kept_ref[0] = dot(t_ref[3 * size :, :], left) + fx_ref[:size, :].astype(F32)
+    kept_ref[1] = dot(t_ref[3 * size :, :], right) + fy_ref[size:, :].astype(F32)
 
 
 def second_kernel(
-    t_ref, q1_ref, q2_ref, key_ref, value_ref, ex_ref, ey_ref, lx_ref, ly_ref, e_ref, o_ref,
-    x_ref, y_ref, kl_ref, kr_ref,
+    even_ref, t_ref, q1_ref, q2_ref, key_ref, value_ref, fx_ref, fy_ref, kept_ref, extra_ref,
+    x_ref, y_ref, both_ref, held_ref, sent_ref,
 ):
     size = t_ref.shape[0] // 4
 
-    def term(place, query_ref, other_ref, extra, early_ref, late_ref, half):
+    def term(place, query_ref, other_ref, extra, from_ref, half):
         block = t_ref[place * size : (place + 1) * size, :]
-        here = slice(half * size, (half + 1) * size)
-        early, late = early_ref[here, :].astype(F32), late_ref[here, :].astype(F32)
-        return jnp.concatenate(
-            [
-                dot(block, query_ref[...]) + early[:, :PAIR],
-                dot(block, other_ref[...]) + late,
-                extra + early[:, PAIR:],
-            ],
-            axis=1,
-        )
-
-    y_ref[...] = term(2, q1_ref, key_ref, e_ref[0], ex_ref, lx_ref, 1).astype(BF)
-    x_ref[...] = term(0, q2_ref, value_ref, o_ref[0], ey_ref, ly_ref, 0).astype(BF)
-    kl_ref[...] = term(3, q1_ref, key_ref, e_ref[1], ex_ref, lx_ref, 0)
-    kr_ref[...] = term(3, q2_ref, value_ref, o_ref[1], ey_ref, ly_ref, 1)
+        value = [dot(block, query_ref[...]), dot(block, other_ref[...]), extra]
+        return jnp.concatenate(value, axis=1) + get_tiles(
+            from_ref, half * size, 2 * size, size, 5
+        )
+
+    y_ref[...] = term(2, q1_ref, key_ref, extra_ref[0], fx_ref, 1).astype(BF)
+    x_ref[...] = term(0, q2_ref, value_ref, extra_ref[2], fy_ref, 0).astype(BF)
+    both_ref[0] = term(3, q1_ref, key_ref, extra_ref[1], fx_ref, 0)
+    both_ref[1] = term(3, q2_ref, value_ref, extra_ref[3], fy_ref, 1)
+    left = kept_ref[0] + get_tiles(fy_ref, 10 * size, size, size, 3)
+    right = kept_ref[1] + get_tiles(fx_ref, 10 * size, size, size, 3)
+    evens = jnp.concatenate([left[:, :PAIR], right[:, : 2 * PAIR]], axis=1)
+    odds = jnp.concatenate([left[:, PAIR:], right[:, 2 * PAIR :]], axis=1)
+    even = even_ref[0] == 1
+    held_ref[...] = jnp.where(even, evens, odds)
+    sent_ref[...] = jnp.where(even, odds, evens).astype(BF)
 
 
 def gate(value, *others):
@@ -522,9 +539,8 @@
     if fast:
         top, low_half = pick_weights(w_qkv, w_out, core_flag)
         far_top, near_low = square(top, 2), square(low_half, 1)
+        near_top, far_low = square(top, 1), square(low_half, 2)
         diag_top, diag_low = square(far_top, 1), square(near_low, 2)
-        later_top, later_low = lax.optimization_barrier((top, low_half, far_top, near_low))[:2]
-        near_top, far_low = square(later_top, 1), square(later_low, 2)
         near, diag = (near_top, near_low), (diag_top, diag_low)
         far, shard = (far_top, far_low), (top, low_half)
         wide = 3 * part_width // 2
@@ -646,7 +662,7 @@
     half = 3 * query_width // 2
     if fast:
         left_0, right_0, to_x, to_y = small_kernel(
-            rim_kernel, "rims_first", [even_flag],
+            first_kernel, "leave_first", [even_flag],
             [normed_t, *rims_0, first[1], first[2], first[3]],
             [((rows, half), BF)] * 2 + [((model_width // 2, half), BF)] * 2,
         )
@@ -663,46 +679,28 @@
     att_1 = fourth[0]
     if fast:
         quarter = model_width // 4
-        key_1, value_1, to_x, to_y = small_kernel(
-            rim_kernel, "rims_second", [even_flag],
-            [normed_t, *rims_1, third[2], fourth[2], third[3], fourth[3]],
-            [((rows, query_width), BF)] * 2 + [((model_width // 2, query_width), BF)] * 2,
-        )
-        late_x, late_y = square(to_x, 1), square(to_y, 2)
-        to_x, to_y, left, right, evens, odds = small_kernel(
-            leave_kernel, "leave_early", [scene_flag],
-            [normed_t, first[7], third[7], fourth[7], gate(chip_cotangent, to_x, to_y), third[1], fourth[1],
-             left_0, right_0, from_x0, from_y0],
-            [((3 * quarter, half), BF)] * 2
-            + [((quarter, half), F32)] * 2
-            + [((2, quarter, quarter), F32)] * 2,
+        tiles = 13 * quarter
+        to_x, to_y, key_1, value_1, kept_0, extra = small_kernel(
+            leave_kernel, "leave", [scene_flag, even_flag],
+            [normed_t, *rims_1, third[2], fourth[2], third[3], fourth[3], first[7], third[7],
+             fourth[7], chip_cotangent, third[1], fourth[1], left_0, right_0, from_x0, from_y0],
+            [((tiles, PAIR), BF)] * 2
+            + [((rows, query_width), BF)] * 2
+            + [((2, quarter, half), F32), ((4, quarter, quarter), F32)],
             [pltpu.VMEM((4, PAIR, rows), BF)],
         )
-        early_x, early_y = square(to_x, 1), square(to_y, 2)
-
-        left_0, key_1, value_1 = lax.optimization_barrier((left_0, key_1, value_1, to_x, to_y))[:3]
+        from_x, from_y = square(to_x, 1), square(to_y, 2)
+        left_0, key_0, att_0, att_1 = lax.optimization_barrier(
+            (left_0, key_1, att_0, att_1, to_x, to_y)
+        )[:4]
         grad_0 = jnp.concatenate([left_0, right_0], axis=1)
-        ngrad_part = dot(grad_0, weights_0, ((1,), (1,))) + dot(
-            jnp.concatenate([third[1], fourth[1], key_1, value_1], axis=1), weights_1, ((1,), (1,))
-        )
-        height = model_width // 4
-        kept_0, sent = groups_of(
-            left + early_y[2 * height :].astype(F32), right + early_x[2 * height :].astype(F32), 0
-        )
-        got_0 = chips(sent, 1, n_vox)
-        to_x, to_y, left, right = small_kernel(
-            second_kernel, "second_exchange", [],
-            [normed_t, third[1], fourth[1], key_1, value_1, early_x, early_y, late_x, late_y, evens, odds],
-            [((height, half + quarter), BF)] * 2 + [((height, half + quarter), F32)] * 2,
-        )
-        end_x, end_y = square(to_x, 1), square(to_y, 2)
-        att_0, att_1, got_0 = lax.optimization_barrier((att_0, att_1, got_0, to_x, to_y))[:3]
+        grad_1 = jnp.concatenate([third[1], fourth[1], key_0, value_1], axis=1)
     else:
         key_1, value_1 = key_value_grads(
             *[jnp.concatenate([third[i], fourth[i]], axis=1) for i in (2, 3)], rims_1
         )
         grad_1 = jnp.concatenate([third[1], fourth[1], key_1, value_1], axis=1)
-        ngrad_part = dot(grad_0, weights_0, ((1,), (1,))) + dot(grad_1, weights_1, ((1,), (1,)))
+    ngrad_part = dot(grad_0, weights_0, ((1,), (1,))) + dot(grad_1, weights_1, ((1,), (1,)))
     mixed_part = dot(att_0, out_rows(CHUNKS[0])) + dot(att_1, out_rows(CHUNKS[1]))
     mixed_mine = lax.dynamic_slice_in_dim(mixed_part, core * own_rows, own_rows, 0)
     mixed_theirs = lax.dynamic_slice_in_dim(mixed_part, (1 - core) * own_rows, own_rows, 0)
@@ -747,25 +745,37 @@
 
     if fast:
         small = jnp.concatenate([gain_grad, scale_grad, jnp.zeros((112,), F32)]).reshape(9, 128)
-        end_x, end_y, small = lax.optimization_barrier((end_x, end_y, small))
+        from_x, from_y, small, mixed_part, _ = lax.optimization_barrier(
+            (from_x, from_y, small, mixed_part, token_grad)
+        )
+        to_x, to_y, both, kept_0, sent = small_kernel(
+            second_kernel, "second_exchange", [even_flag],
+            [normed_t, third[1], fourth[1], key_1, value_1, from_x, from_y, kept_0, extra],
+            [((quarter, half + quarter), BF)] * 2
+            + [((2, quarter, half + quarter), F32), ((quarter, half), F32), ((quarter, half), BF)],
+        )
+        end_x, end_y = square(to_x, 1), square(to_y, 2)
+        sent, small = lax.optimization_barrier((sent, small, to_x, to_y))[:2]
+        got_0 = chips(sent, 1, n_vox)
         small = small + square(small, 1)
+        kept_1, sent = groups_of(both[0] + end_y.astype(F32), both[1] + end_x.astype(F32), 1)
+        got_1 = chips(sent, 1, n_vox)
+        small, got_0 = lax.optimization_barrier((small, got_0, sent))[:2]
+        small = small + square(small, 2)
+        small = small + lax.ppermute(small, "vox", swap)
         kept_0, sent = halves_of(kept_0 + got_0.astype(F32))
         got_0 = chips(sent, 2, n_vox)
-        kept_1, sent = groups_of(left + end_y.astype(F32), right + end_x.astype(F32), 1)
-        got_1 = chips(sent, 1, n_vox)
-        small = gate(small, sent)
-        small = small + square(small, 2)
-        small = small + lax.ppermute(small, "vox", swap)
-        got_1, small, token_grad = lax.optimization_barrier((got_1, small, token_grad))
+        got_1, small = lax.optimization_barrier((got_1, small))
         kept_1, sent = halves_of(kept_1 + got_1.astype(F32))
         got_1 = chips(sent, 2, n_vox)
         small = gate(small, sent)
         small = small + chips(small, 1, n_vox)
         small = small + chips(small, 2, n_vox)
-        got_1, small, mixed = lax.optimization_barrier((got_1, small, mixed))
+        got_1, small = lax.optimization_barrier((got_1, small))
         small = small.reshape(-1)
         summed_gain, summed_scale = small[:model_width], small[model_width : model_width + HEADS]
         kept_1 = kept_1 + got_1.astype(F32)
+        height = model_width // 4
         qkv_sums = [kept_0 + got_0.astype(F32), kept_1[:height]]
         out_sum = kept_1[height:]
     else:

time: 186 us -> 193 us (1.038)
  local copies, waits for them, and re-layouts: 28.6 us -> 35.4 us
  other arithmetic: 18.5 us -> 14.3 us
  Pallas kernels: 29.5 us -> 33.2 us
    unnamed x157 -> x161, local copies, waits for them, and re-layouts: 21.1 us -> 26.4 us
    ppermute x16 -> x14, waiting for transfers between devices: 38.2 us -> 41.9 us  [square(): return lax.ppermute(value, 'fsdp', [(i, i ^ step) for i in range(4)])]
    ppermute x3, waiting for transfers between devices: 8.25 us -> 4.83 us  [pairings(): lax.ppermute(first, 'vox', near_chips)]
    pallas_call x6 -> x5, Pallas kernels: 6.23 us -> 9.18 us  [small_kernel(): pl.pallas_call(kernel, grid_spec=pltpu.PrefetchScalarGridSpec(num_scalar_...]
    ppermute x6, starting transfers between devices: 10.2 us -> 12.8 us  [chips(): return lax.ppermute(value, 'vox', [(i, i ^ 2 * step) for i in range(n_vox)])]
    ppermute x16 -> x14, starting transfers between devices: 17.8 us -> 15.4 us  [square(): return lax.ppermute(value, 'fsdp', [(i, i ^ step) for i in range(4)])]
    ppermute x3, starting transfers between devices: 2.67 us -> 4.73 us  [pairings(): lax.ppermute(second, 'vox', far_chips)]
  transfers between devices with their start and end apart: 36 -> 34, of which waited for: 15 -> 13; matrix products, arithmetic and copies ran while one was open for 17% -> 13% of each run, Pallas kernels for 7% -> 7%
where the time goes in v2:
time: 193 us; the launch traced here: 192 us
  waiting for transfers between devices  57.2 us (30%)
  starting transfers between devices  42.4 us (22%)
  local copies, waits for them, and re-layouts  35.4 us (18%)
  Pallas kernels  33.2 us (17%)
  other arithmetic  14.3 us (7%)
  matrix products  7.81 us (4%)
    ppermute x14, waiting for transfers between devices, square(): return lax.ppermute(value, 'fsdp', [(i, i ^ step) for i in range(4)])  41.9 us
    unnamed x161, local copies, waits for them, and re-layouts  26.4 us
    pallas_call x3, Pallas kernels, attention(): pl.pallas_call(attention_kernel, grid_spec=pltpu.PrefetchScalarGridSpec(n...  24 us
    ppermute x14, starting transfers between devices, square(): return lax.ppermute(value, 'fsdp', [(i, i ^ step) for i in range(4)])  15.4 us
    ppermute x6, starting transfers between devices, chips(): return lax.ppermute(value, 'vox', [(i, i ^ 2 * step) for i in range(n_vox)])  12.8 us
    ppermute x6, waiting for transfers between devices, chips(): return lax.ppermute(value, 'vox', [(i, i ^ 2 * step) for i in range(n_vox)])  9.85 us
    pallas_call x5, Pallas kernels, small_kernel(): pl.pallas_call(kernel, grid_spec=pltpu.PrefetchScalarGridSpec(num_scalar_...  9.18 us
    ppermute x3, starting transfers between devices, pairings(): lax.ppermute(first, 'vox', near_chips)  8.22 us
  transfers between devices with their start and end apart: 34, of which 13 were waited for; matrix products, arithmetic and copies ran while one was open for 13% of the time, Pallas kernels for 7%

profile of v2, /device:TPU:0, one launch (start us, length us, event | category | flops | bytes accessed | tf_op | source)
XLA Modules:
  0.0 192.1 jit_solution(14786841283977836907)
XLA Ops:
  3.4 3.0 %collective-permute-start.4 = (bf16[128,2048]{1,0:T(8,128)(2,1)S(1)}, bf16[128,2048]{1,0:T(8,128)(2,1)}, u32[]{:S(2)}, u32[]{:S(2)}) collective-permute-start(bf16[128,2048]{1,0:T(8,128)(2,1)S(1)} %get-tuple-element.68), channel_id=1, source_target_pairs={{0,2},{1,3},{2,0},{3,1},{4,6},{5,7},{6,4},{7,5},{8,10},{9,11},{10,... | collective-permute-start | bytes 1572872 | tf_op jit(solution)/shard_map/ppermute | solution.py:489
  11.7 7.5 %collective-permute-done.4 = bf16[128,2048]{1,0:T(8,128)(2,1)} collective-permute-done((bf16[128,2048]{1,0:T(8,128)(2,1)S(1)}, bf16[128,2048]{1,0:T(8,128)(2,1)}, u32[]{:S(2)}, u32[]{:S(2)}) %collective-permute-start.4) | collective-permute-done | bytes 524320 | tf_op jit(solution)/shard_map/ppermute | solution.py:489
  20.2 10.9 %collective-permute-done.3 = bf16[128,2048]{1,0:T(8,128)(2,1)} collective-permute-done((bf16[128,2048]{1,0:T(8,128)(2,1)S(1)}, bf16[128,2048]{1,0:T(8,128)(2,1)}, u32[]{:S(2)}, u32[]{:S(2)}) %collective-permute-start.3) | collective-permute-done | bytes 524320 | tf_op jit(solution)/shard_map/ppermute | solution.py:489
  40.8 3.1 %collective-permute-done.5 = bf16[128,2048]{1,0:T(8,128)(2,1)S(1)} collective-permute-done((bf16[128,2048]{1,0:T(8,128)(2,1)}, bf16[128,2048]{1,0:T(8,128)(2,1)S(1)}, u32[]{:S(2)}, u32[]{:S(2)}) %collective-permute-start.5) | collective-permute-done | bytes 524320 | tf_op jit(solution)/shard_map/ppermute | solution.py:489
  43.8 2.2 %collective-permute-done.6 = bf16[128,2048]{1,0:T(8,128)(2,1)S(1)} collective-permute-done((bf16[128,2048]{1,0:T(8,128)(2,1)}, bf16[128,2048]{1,0:T(8,128)(2,1)S(1)}, u32[]{:S(2)}, u32[]{:S(2)}) %collective-permute-start.6) | collective-permute-done | bytes 524320 | tf_op jit(solution)/shard_map/ppermute | solution.py:489
  51.4 4.4 %collective-permute-start.8 = (bf16[192,1024]{1,0:T(8,128)(2,1)S(1)}, bf16[192,1024]{1,0:T(8,128)(2,1)S(1)}, u32[]{:S(2)}, u32[]{:S(2)}) collective-permute-start(bf16[192,1024]{1,0:T(8,128)(2,1)S(1)} %get-tuple-element.161), channel_id=1, source_target_pairs={{0,8},{4,12},{8,0},{12,4},{16,24},{20,28},{24,16},{28,20},{1,9},{5... | collective-permute-start | bytes 1179656 | tf_op jit(solution)/shard_map/ppermute | solution.py:604
  57.5 4.8 %collective-permute-done.8.k1_ref.v1_ref = bf16[192,1024]{1,0:T(8,128)(2,1)S(1)} collective-permute-done((bf16[192,1024]{1,0:T(8,128)(2,1)S(1)}, bf16[192,1024]{1,0:T(8,128)(2,1)S(1)}, u32[]{:S(2)}, u32[]{:S(2)}) %collective-permute-start.8) | collective-permute-done | bytes 393248 | tf_op jit(solution)/shard_map/ppermute | solution.py:604
  62.3 11.8 %block_attention.3 = (bf16[768,256]{1,0:T(8,128)(2,1)S(1)}, bf16[768,256]{1,0:T(8,128)(2,1)S(1)}, f32[768,256]{1,0:T(8,128)S(1)}, f32[768,256]{1,0:T(8,128)S(1)}...) custom-call(s32[12,8]{1,0:T(8,128)S(1)} %copy.23.mult_ref, ...), custom_call_target="tpu_custom_call" | custom-call | flops 19327352832 | bytes 3932160 | tf_op jit(solution)/shard_map/block_attention/pallas_call | solution.py:216
  74.1 1.8 collective-permute-start.11
  76.8 5.7 %block_attention.4 = (bf16[768,128]{1,0:T(8,128)(2,1)S(1)}, bf16[768,128]{1,0:T(8,128)(2,1)S(1)}, f32[768,128]{1,0:T(8,128)S(1)}, f32[768,128]{1,0:T(8,128)S(1)}...) custom-call(s32[12,8]{1,0:T(8,128)S(1)} %copy.23.mult_ref, ...), custom_call_target="tpu_custom_call" | custom-call | flops 9663676416 | bytes 1966080 | tf_op jit(solution)/shard_map/block_attention/pallas_call | solution.py:216
  83.3 1.8 leave_first.1
  86.2 6.5 %block_attention.5 = (bf16[768,256]{1,0:T(8,128)(2,1)S(1)}, bf16[768,128]{1,0:T(8,128)(2,1)S(1)}, f32[768,128]{1,0:T(8,128)S(1)}, f32[768,128]{1,0:T(8,128)S(1)}...) custom-call(s32[12,8]{1,0:T(8,128)S(1)} %copy.23.mult_ref, ...), custom_call_target="tpu_custom_call" | custom-call | flops 9663676416 | bytes 1966080 | tf_op jit(solution)/shard_map/block_attention/pallas_call | solution.py:216
  95.1 2.0 %collective-permute-start.13 = (bf16[2,192,256]{2,1,0:T(8,128)(2,1)}, bf16[2,192,256]{2,1,0:T(8,128)(2,1)}, u32[]{:S(2)}, u32[]{:S(2)}) collective-permute-start(bf16[2,192,256]{2,1,0:T(8,128)(2,1)} %get-tuple-element.86), channel_id=1, source_target_pairs={{0,8},{4,12},{8,0},{12,4},{16,24},{20,28},{24,16},{28,20},{1,9},{5... | collective-permute-start | bytes 589832 | tf_op jit(solution)/shard_map/ppermute | solution.py:604
  97.0 3.0 %collective-permute-start.14 = (bf16[2,192,256]{2,1,0:T(8,128)(2,1)}, bf16[2,192,256]{2,1,0:T(8,128)(2,1)}, u32[]{:S(2)}, u32[]{:S(2)}) collective-permute-start(bf16[2,192,256]{2,1,0:T(8,128)(2,1)} %get-tuple-element.87), channel_id=1, source_target_pairs={{0,0},{4,4},{8,16},{12,20},{16,8},{20,12},{24,24},{28,28},{1,1},{5... | collective-permute-start | bytes 589832 | tf_op jit(solution)/shard_map/ppermute | solution.py:604
  100.1 1.6 pad_maximum_fusion.2.cot_ref
  102.0 4.9 %leave.1 = (bf16[3328,128]{1,0:T(8,128)(2,1)}, bf16[3328,128]{1,0:T(8,128)(2,1)S(1)}, bf16[768,256]{1,0:T(8,128)(2,1)S(1)}, bf16[768,256]{1,0:T(8,128)(2,1)S(1)}...) custom-call(s32[1]{0:T(128)} %bitcast.9.scene_ref, s32[1]{0:T(128)} %bitcast.1.even_ref, ...), custom_call_target="tpu_custom_call" | custom-call | tf_op jit(solution)/shard_map/leave/pallas_call | solution.py:303
  117.5 1.5 collective-permute-start.19
  119.1 1.5 collective-permute-start.20
  120.6 2.2 %dynamic-slice_add_fusion = f32[384,1024]{1,0:T(8,128)S(1)} fusion(f32[384,1024]{1,0:T(8,128)} %collective-permute-done.18, f32[768,1024]{1,0:T(8,128)} %copy-done.40, s32[]{:T(128)S(6)} %select_n.443), kind=kLoop, calls=%fused_computation.26 | loop fusion | flops 393216 | bytes 4718596 | tf_op jit(solution)/shard_map/add | solution.py:713
  123.0 2.2 %copy-done.39 = f32[768,1024]{1,0:T(8,128)S(1)} copy-done((f32[768,1024]{1,0:T(8,128)S(1)}, f32[768,1024]{1,0:T(8,128)}, u32[]{:S(2)}) %copy-start.39) | copy-done | bytes 3145752
  125.3 2.8 %fusion.7 = (f32[1024]{0:T(1024)S(1)}, f32[384]{0:T(512)S(1)}, bf16[1,384,1024]{2,1,0:T(8,128)(2,1)}) fusion(f32[384,256]{1,0:T(8,128)S(1)} %get-tuple-element.140, f32[384,256]{1,0:T(8,128)S(1)} %get-tuple-element.139, f32[384,256]{1,0:T(8,128)S(1)} %get-tuple-element.138, f32[384,256]{1,0:T(8,128)S(1)} %get-tuple-element.137, f32[384]{0:T(512)S(1)} %add_rsqrt_fusion.1, ...), kind=kLoop, calls=%fused_computation.16 | loop fusion | flops 5110400 | bytes 6302724 | tf_op jit(solution)/shard_map/reduce_sum | solution.py:722
  128.2 11.0 %collective-permute-done.19.fx_ref = bf16[3328,128]{1,0:T(8,128)(2,1)S(1)} collective-permute-done((bf16[3328,128]{1,0:T(8,128)(2,1)}, bf16[3328,128]{1,0:T(8,128)(2,1)S(1)}, u32[]{:S(2)}, u32[]{:S(2)}) %collective-permute-start.19) | collective-permute-done | bytes 852000 | tf_op jit(solution)/shard_map/ppermute | solution.py:489
  148.9 1.8 second_exchange.1
  152.1 1.5 collective-permute-start.21
  155.7 3.0 %collective-permute-start.25 = (bf16[256,384]{1,0:T(8,128)(2,1)}, bf16[256,384]{1,0:T(8,128)(2,1)S(1)}, u32[]{:S(2)}, u32[]{:S(2)}) collective-permute-start(bf16[256,384]{1,0:T(8,128)(2,1)} %copy-done.37), channel_id=1, source_target_pairs={{0,8},{4,12},{8,0},{12,4},{16,24},{20,28},{24,16},{28,20},{1,9},{5... | collective-permute-start | bytes 589832 | tf_op jit(solution)/shard_map/ppermute | solution.py:493
  158.7 3.9 %collective-permute-done.24 = f32[9,128]{1,0:T(8,128)S(1)} collective-permute-done((f32[9,128]{1,0:T(8,128)S(1)}, f32[9,128]{1,0:T(8,128)S(1)}, u32[]{:S(2)}, u32[]{:S(2)}) %collective-permute-start.24) | collective-permute-done | bytes 4640 | tf_op jit(solution)/shard_map/ppermute | solution.py:489
  163.0 3.1 %collective-permute-start.23 = (bf16[256,640]{1,0:T(8,128)(2,1)S(1)}, bf16[256,640]{1,0:T(8,128)(2,1)S(1)}, u32[]{:S(2)}, u32[]{:S(2)}) collective-permute-start(bf16[256,640]{1,0:T(8,128)(2,1)S(1)} %select_convert_fusion), channel_id=1, source_target_pairs={{0,8},{4,12},{8,0},{12,4},{16,24},{20,28},{24,16},{28,20},{1,9},{5... | collective-permute-start | bytes 983048 | tf_op jit(solution)/shard_map/ppermute | solution.py:493
  166.6 3.1 %collective-permute-done.26 = f32[9,128]{1,0:T(8,128)S(1)} collective-permute-done((f32[9,128]{1,0:T(8,128)S(1)}, f32[9,128]{1,0:T(8,128)S(1)}, u32[]{:S(2)}, u32[]{:S(2)}) %collective-permute-start.26) | collective-permute-done | bytes 4640 | tf_op jit(solution)/shard_map/ppermute | solution.py:489
  172.5 1.8 collective-permute-start.29
  175.8 3.1 %collective-permute-start.28 = (bf16[384,256]{1,0:T(8,128)(2,1)S(1)}, bf16[384,256]{1,0:T(8,128)(2,1)S(1)}, u32[]{:S(2)}, u32[]{:S(2)}) collective-permute-start(bf16[384,256]{1,0:T(8,128)(2,1)S(1)} %select_convert_fusion.1), channel_id=1, source_target_pairs={{0,16},{4,20},{8,24},{12,28},{16,0},{20,4},{24,8},{28,12},{1,17},{... | collective-permute-start | bytes 589832 | tf_op jit(solution)/shard_map/ppermute | solution.py:493
  179.5 4.4 %collective-permute-done.31 = bf16[256,256]{1,0:T(8,128)(2,1)S(1)} collective-permute-done((bf16[256,256]{1,0:T(8,128)(2,1)S(1)}, bf16[256,256]{1,0:T(8,128)(2,1)S(1)}, u32[]{:S(2)}, u32[]{:S(2)}) %collective-permute-start.31) | collective-permute-done | bytes 131104 | tf_op jit(solution)/shard_map/ppermute | solution.py:493
  184.0 4.1 %collective-permute-done.30 = f32[9,128]{1,0:T(8,128)S(1)} collective-permute-done((f32[9,128]{1,0:T(8,128)S(1)}, f32[9,128]{1,0:T(8,128)S(1)}, u32[]{:S(2)}, u32[]{:S(2)}) %collective-permute-start.30) | collective-permute-done | bytes 4640 | tf_op jit(solution)/shard_map/ppermute | solution.py:493
  (295 shorter events, 64.1 us)
Async XLA Ops:
  3.4 15.9 %collective-permute-start.4 = (bf16[128,2048]{1,0:T(8,128)(2,1)S(1)}, bf16[128,2048]{1,0:T(8,128)(2,1)}, u32[]{:S(2)}, u32[]{:S(2)}) collective-permute-start(bf16[128,2048]{1,0:T(8,128)(2,1)S(1)} %get-tuple-element.68), channel_id=1, source_target_pairs={{0,2},{1,3},{2,0},{3,1},{4,6},{5,7},{6,4},{7,5},{8,10},{9,11},{10,... | collective-permute-start | bytes 1572872 | tf_op jit(solution)/shard_map/ppermute | solution.py:489
  6.4 27.1 %collective-permute-start.2 = (bf16[128,2048]{1,0:T(8,128)(2,1)S(1)}, bf16[128,2048]{1,0:T(8,128)(2,1)}, u32[]{:S(2)}, u32[]{:S(2)}) collective-permute-start(bf16[128,2048]{1,0:T(8,128)(2,1)S(1)} %get-tuple-element.68), channel_id=1, source_target_pairs={{0,1},{1,0},{2,3},{3,2},{4,5},{5,4},{6,7},{7,6},{8,9},{9,8},{10,11... | collective-permute-start | bytes 1572872 | tf_op jit(solution)/shard_map/ppermute | solution.py:489
  7.9 27.1 %collective-permute-start.7 = (bf16[128,2048]{1,0:T(8,128)(2,1)S(1)}, bf16[128,2048]{1,0:T(8,128)(2,1)S(1)}, u32[]{:S(2)}, u32[]{:S(2)}) collective-permute-start(bf16[128,2048]{1,0:T(8,128)(2,1)S(1)} %get-tuple-element.69), channel_id=1, source_target_pairs={{0,2},{1,3},{2,0},{3,1},{4,6},{5,7},{6,4},{7,5},{8,10},{9,11},{10,... | collective-permute-start | bytes 1572872 | tf_op jit(solution)/shard_map/ppermute | solution.py:489
  8.4 22.7 %collective-permute-start.3 = (bf16[128,2048]{1,0:T(8,128)(2,1)S(1)}, bf16[128,2048]{1,0:T(8,128)(2,1)}, u32[]{:S(2)}, u32[]{:S(2)}) collective-permute-start(bf16[128,2048]{1,0:T(8,128)(2,1)S(1)} %get-tuple-element.69), channel_id=1, source_target_pairs={{0,1},{1,0},{2,3},{3,2},{4,5},{5,4},{6,7},{7,6},{8,9},{9,8},{10,11... | collective-permute-start | bytes 1572872 | tf_op jit(solution)/shard_map/ppermute | solution.py:489
  8.6 2.4 %collective-permute-start.1 = (f32[6,9]{0,1:T(8,128)S(1)}, f32[6,9]{0,1:T(8,128)S(1)}, u32[]{:S(2)}, u32[]{:S(2)}) collective-permute-start(f32[6,9]{0,1:T(8,128)S(1)} %fusion.42), channel_id=1, source_target_pairs={{0,4},{4,0},{8,12},{12,8},{16,20},{20,16},{24,28},{28,24},{1,5},{5... | collective-permute-start | bytes 656 | tf_op jit(solution)/shard_map/ppermute | solution.py:573
  11.0 26.4 %collective-permute-start = (bf16[384,1024]{1,0:T(8,128)(2,1)S(1)}, bf16[384,1024]{1,0:T(8,128)(2,1)}, u32[]{:S(2)}, u32[]{:S(2)}) collective-permute-start(bf16[384,1024]{1,0:T(8,128)(2,1)S(1)} %bitcast.57), channel_id=1, source_target_pairs={{0,4},{4,0},{8,12},{12,8},{16,20},{20,16},{24,28},{28,24},{1,5},{5... | collective-permute-start | bytes 2359304 | tf_op jit(solution)/shard_map/ppermute | solution.py:569
  19.3 21.3 %collective-permute-start.10 = (bf16[384,1024]{1,0:T(8,128)(2,1)S(1)}, bf16[384,1024]{1,0:T(8,128)(2,1)S(1)}, u32[]{:S(2)}, u32[]{:S(2)}) collective-permute-start(bf16[384,1024]{1,0:T(8,128)(2,1)S(1)} %bitcast.62), channel_id=1, source_target_pairs={{0,4},{4,0},{8,12},{12,8},{16,20},{20,16},{24,28},{28,24},{1,5},{5... | collective-permute-start | bytes 2359304 | tf_op jit(solution)/shard_map/ppermute | solution.py:570
  31.1 12.7 %collective-permute-start.5 = (bf16[128,2048]{1,0:T(8,128)(2,1)}, bf16[128,2048]{1,0:T(8,128)(2,1)S(1)}, u32[]{:S(2)}, u32[]{:S(2)}) collective-permute-start(bf16[128,2048]{1,0:T(8,128)(2,1)} %collective-permute-done.4), channel_id=1, source_target_pairs={{0,1},{1,0},{2,3},{3,2},{4,5},{5,4},{6,7},{7,6},{8,9},{9,8},{10,11... | collective-permute-start | bytes 1572872 | tf_op jit(solution)/shard_map/ppermute | solution.py:489
  33.5 12.5 %collective-permute-start.6 = (bf16[128,2048]{1,0:T(8,128)(2,1)}, bf16[128,2048]{1,0:T(8,128)(2,1)S(1)}, u32[]{:S(2)}, u32[]{:S(2)}) collective-permute-start(bf16[128,2048]{1,0:T(8,128)(2,1)} %collective-permute-done.3), channel_id=1, source_target_pairs={{0,2},{1,3},{2,0},{3,1},{4,6},{5,7},{6,4},{7,5},{8,10},{9,11},{10,... | collective-permute-start | bytes 1572872 | tf_op jit(solution)/shard_map/ppermute | solution.py:489
  50.6 6.9 %collective-permute-start.9 = (bf16[192,1024]{1,0:T(8,128)(2,1)S(1)}, bf16[192,1024]{1,0:T(8,128)(2,1)S(1)}, u32[]{:S(2)}, u32[]{:S(2)}) collective-permute-start(bf16[192,1024]{1,0:T(8,128)(2,1)S(1)} %get-tuple-element.160), channel_id=1, source_target_pairs={{0,0},{4,4},{8,16},{12,20},{16,8},{20,12},{24,24},{28,28},{1,1},{5... | collective-permute-start | bytes 1179656 | tf_op jit(solution)/shard_map/ppermute | solution.py:604
  51.4 10.9 %collective-permute-start.8 = (bf16[192,1024]{1,0:T(8,128)(2,1)S(1)}, bf16[192,1024]{1,0:T(8,128)(2,1)S(1)}, u32[]{:S(2)}, u32[]{:S(2)}) collective-permute-start(bf16[192,1024]{1,0:T(8,128)(2,1)S(1)} %get-tuple-element.161), channel_id=1, source_target_pairs={{0,8},{4,12},{8,0},{12,4},{16,24},{20,28},{24,16},{28,20},{1,9},{5... | collective-permute-start | bytes 1179656 | tf_op jit(solution)/shard_map/ppermute | solution.py:604
  74.1 9.2 %collective-permute-start.11 = (bf16[2,192,256]{2,1,0:T(8,128)(2,1)S(1)}, bf16[2,192,256]{2,1,0:T(8,128)(2,1)S(1)}, u32[]{:S(2)}, u32[]{:S(2)}) collective-permute-start(bf16[2,192,256]{2,1,0:T(8,128)(2,1)S(1)} %get-tuple-element.70), channel_id=1, source_target_pairs={{0,8},{4,12},{8,0},{12,4},{16,24},{20,28},{24,16},{28,20},{1,9},{5... | collective-permute-start | bytes 589832 | tf_op jit(solution)/shard_map/ppermute | solution.py:604
  75.9 7.4 %collective-permute-start.12 = (bf16[2,192,256]{2,1,0:T(8,128)(2,1)S(1)}, bf16[2,192,256]{2,1,0:T(8,128)(2,1)S(1)}, u32[]{:S(2)}, u32[]{:S(2)}) collective-permute-start(bf16[2,192,256]{2,1,0:T(8,128)(2,1)S(1)} %get-tuple-element.71), channel_id=1, source_target_pairs={{0,0},{4,4},{8,16},{12,20},{16,8},{20,12},{24,24},{28,28},{1,1},{5... | collective-permute-start | bytes 589832 | tf_op jit(solution)/shard_map/ppermute | solution.py:604
  85.2 16.6 %collective-permute-start.15 = (bf16[512,384]{1,0:T(8,128)(2,1)}, bf16[512,384]{1,0:T(8,128)(2,1)}, u32[]{:S(2)}, u32[]{:S(2)}) collective-permute-start(bf16[512,384]{1,0:T(8,128)(2,1)} %get-tuple-element.80), channel_id=1, source_target_pairs={{0,1},{1,0},{2,3},{3,2},{4,5},{5,4},{6,7},{7,6},{8,9},{9,8},{10,11... | collective-permute-start | bytes 1179656 | tf_op jit(solution)/shard_map/ppermute | solution.py:489
  85.7 16.0 %collective-permute-start.16 = (bf16[512,384]{1,0:T(8,128)(2,1)}, bf16[512,384]{1,0:T(8,128)(2,1)}, u32[]{:S(2)}, u32[]{:S(2)}) collective-permute-start(bf16[512,384]{1,0:T(8,128)(2,1)} %get-tuple-element.81), channel_id=1, source_target_pairs={{0,2},{1,3},{2,0},{3,1},{4,6},{5,7},{6,4},{7,5},{8,10},{9,11},{10,... | collective-permute-start | bytes 1179656 | tf_op jit(solution)/shard_map/ppermute | solution.py:489
  95.1 6.6 %collective-permute-start.13 = (bf16[2,192,256]{2,1,0:T(8,128)(2,1)}, bf16[2,192,256]{2,1,0:T(8,128)(2,1)}, u32[]{:S(2)}, u32[]{:S(2)}) collective-permute-start(bf16[2,192,256]{2,1,0:T(8,128)(2,1)} %get-tuple-element.86), channel_id=1, source_target_pairs={{0,8},{4,12},{8,0},{12,4},{16,24},{20,28},{24,16},{28,20},{1,9},{5... | collective-permute-start | bytes 589832 | tf_op jit(solution)/shard_map/ppermute | solution.py:604
  97.0 4.7 %collective-permute-start.14 = (bf16[2,192,256]{2,1,0:T(8,128)(2,1)}, bf16[2,192,256]{2,1,0:T(8,128)(2,1)}, u32[]{:S(2)}, u32[]{:S(2)}) collective-permute-start(bf16[2,192,256]{2,1,0:T(8,128)(2,1)} %get-tuple-element.87), channel_id=1, source_target_pairs={{0,0},{4,4},{8,16},{12,20},{16,8},{20,12},{24,24},{28,28},{1,1},{5... | collective-permute-start | bytes 589832 | tf_op jit(solution)/shard_map/ppermute | solution.py:604
  113.1 7.5 %collective-permute-start.18 = (f32[384,1024]{1,0:T(8,128)}, f32[384,1024]{1,0:T(8,128)}, u32[]{:S(2)}, u32[]{:S(2)}) collective-permute-start(f32[384,1024]{1,0:T(8,128)} %constant_dynamic-slice_fusion), channel_id=1, source_target_pairs={{0,4},{4,0},{8,12},{12,8},{16,20},{20,16},{24,28},{28,24},{1,5},{5... | collective-permute-start | bytes 4718600 | tf_op jit(solution)/shard_map/ppermute | solution.py:713
  117.0 6.0 %collective-permute-start.17 = (f32[384,1024]{1,0:T(8,128)}, f32[384,1024]{1,0:T(8,128)}, u32[]{:S(2)}, u32[]{:S(2)}) collective-permute-start(f32[384,1024]{1,0:T(8,128)} %constant_dynamic-slice_fusion.1), channel_id=1, source_target_pairs={{0,4},{4,0},{8,12},{12,8},{16,20},{20,16},{24,28},{28,24},{1,5},{5... | collective-permute-start | bytes 4718600 | tf_op jit(solution)/shard_map/ppermute | solution.py:708
  117.5 21.6 %collective-permute-start.19 = (bf16[3328,128]{1,0:T(8,128)(2,1)}, bf16[3328,128]{1,0:T(8,128)(2,1)S(1)}, u32[]{:S(2)}, u32[]{:S(2)}) collective-permute-start(bf16[3328,128]{1,0:T(8,128)(2,1)} %get-tuple-element.103), channel_id=1, source_target_pairs={{0,1},{1,0},{2,3},{3,2},{4,5},{5,4},{6,7},{7,6},{8,9},{9,8},{10,11... | collective-permute-start | bytes 2555912 | tf_op jit(solution)/shard_map/ppermute | solution.py:489
  119.1 21.3 %collective-permute-start.20 = (bf16[3328,128]{1,0:T(8,128)(2,1)}, bf16[3328,128]{1,0:T(8,128)(2,1)S(1)}, u32[]{:S(2)}, u32[]{:S(2)}) collective-permute-start(bf16[3328,128]{1,0:T(8,128)(2,1)} %copy-done.36), channel_id=1, source_target_pairs={{0,2},{1,3},{2,0},{3,1},{4,6},{5,7},{6,4},{7,5},{8,10},{9,11},{10,... | collective-permute-start | bytes 2555912 | tf_op jit(solution)/shard_map/ppermute | solution.py:489
  152.1 10.5 %collective-permute-start.21 = (bf16[256,640]{1,0:T(8,128)(2,1)}, bf16[256,640]{1,0:T(8,128)(2,1)S(1)}, u32[]{:S(2)}, u32[]{:S(2)}) collective-permute-start(bf16[256,640]{1,0:T(8,128)(2,1)} %get-tuple-element.116), channel_id=1, source_target_pairs={{0,2},{1,3},{2,0},{3,1},{4,6},{5,7},{6,4},{7,5},{8,10},{9,11},{10,... | collective-permute-start | bytes 983048 | tf_op jit(solution)/shard_map/ppermute | solution.py:489
  153.6 9.0 %collective-permute-start.22 = (bf16[256,640]{1,0:T(8,128)(2,1)S(1)}, bf16[256,640]{1,0:T(8,128)(2,1)S(1)}, u32[]{:S(2)}, u32[]{:S(2)}) collective-permute-start(bf16[256,640]{1,0:T(8,128)(2,1)S(1)} %get-tuple-element.117), channel_id=1, source_target_pairs={{0,1},{1,0},{2,3},{3,2},{4,5},{5,4},{6,7},{7,6},{8,9},{9,8},{10,11... | collective-permute-start | bytes 983048 | tf_op jit(solution)/shard_map/ppermute | solution.py:489
  154.8 7.7 %collective-permute-start.24 = (f32[9,128]{1,0:T(8,128)S(1)}, f32[9,128]{1,0:T(8,128)S(1)}, u32[]{:S(2)}, u32[]{:S(2)}) collective-permute-start(f32[9,128]{1,0:T(8,128)S(1)} %bitcast.65), channel_id=1, source_target_pairs={{0,1},{1,0},{2,3},{3,2},{4,5},{5,4},{6,7},{7,6},{8,9},{9,8},{10,11... | collective-permute-start | bytes 13832 | tf_op jit(solution)/shard_map/ppermute | solution.py:489
  155.7 10.4 %collective-permute-start.25 = (bf16[256,384]{1,0:T(8,128)(2,1)}, bf16[256,384]{1,0:T(8,128)(2,1)S(1)}, u32[]{:S(2)}, u32[]{:S(2)}) collective-permute-start(bf16[256,384]{1,0:T(8,128)(2,1)} %copy-done.37), channel_id=1, source_target_pairs={{0,8},{4,12},{8,0},{12,4},{16,24},{20,28},{24,16},{28,20},{1,9},{5... | collective-permute-start | bytes 589832 | tf_op jit(solution)/shard_map/ppermute | solution.py:493
  163.0 9.2 %collective-permute-start.23 = (bf16[256,640]{1,0:T(8,128)(2,1)S(1)}, bf16[256,640]{1,0:T(8,128)(2,1)S(1)}, u32[]{:S(2)}, u32[]{:S(2)}) collective-permute-start(bf16[256,640]{1,0:T(8,128)(2,1)S(1)} %select_convert_fusion), channel_id=1, source_target_pairs={{0,8},{4,12},{8,0},{12,4},{16,24},{20,28},{24,16},{28,20},{1,9},{5... | collective-permute-start | bytes 983048 | tf_op jit(solution)/shard_map/ppermute | solution.py:493
  166.1 3.7 %collective-permute-start.26 = (f32[9,128]{1,0:T(8,128)S(1)}, f32[9,128]{1,0:T(8,128)S(1)}, u32[]{:S(2)}, u32[]{:S(2)}) collective-permute-start(f32[9,128]{1,0:T(8,128)S(1)} %add.160), channel_id=1, source_target_pairs={{0,2},{1,3},{2,0},{3,1},{4,6},{5,7},{6,4},{7,5},{8,10},{9,11},{10,... | collective-permute-start | bytes 13832 | tf_op jit(solution)/shard_map/ppermute | solution.py:489
  169.8 14.2 %collective-permute-start.31 = (bf16[256,256]{1,0:T(8,128)(2,1)S(1)}, bf16[256,256]{1,0:T(8,128)(2,1)S(1)}, u32[]{:S(2)}, u32[]{:S(2)}) collective-permute-start(bf16[256,256]{1,0:T(8,128)(2,1)S(1)} %select_convert_fusion.2), channel_id=1, source_target_pairs={{0,16},{4,20},{8,24},{12,28},{16,0},{20,4},{24,8},{28,12},{1,17},{... | collective-permute-start | bytes 393224 | tf_op jit(solution)/shard_map/ppermute | solution.py:493
  172.5 6.3 %collective-permute-start.29 = (f32[9,128]{1,0:T(8,128)S(1)}, f32[9,128]{1,0:T(8,128)S(1)}, u32[]{:S(2)}, u32[]{:S(2)}) collective-permute-start(f32[9,128]{1,0:T(8,128)S(1)} %add.162), channel_id=1, source_target_pairs={{0,8},{4,12},{8,0},{12,4},{16,24},{20,28},{24,16},{28,20},{1,9},{5... | collective-permute-start | bytes 13832 | tf_op jit(solution)/shard_map/ppermute | solution.py:493
  175.8 12.4 %collective-permute-start.28 = (bf16[384,256]{1,0:T(8,128)(2,1)S(1)}, bf16[384,256]{1,0:T(8,128)(2,1)S(1)}, u32[]{:S(2)}, u32[]{:S(2)}) collective-permute-start(bf16[384,256]{1,0:T(8,128)(2,1)S(1)} %select_convert_fusion.1), channel_id=1, source_target_pairs={{0,16},{4,20},{8,24},{12,28},{16,0},{20,4},{24,8},{28,12},{1,17},{... | collective-permute-start | bytes 589832 | tf_op jit(solution)/shard_map/ppermute | solution.py:493
  178.8 9.3 %collective-permute-start.30 = (f32[9,128]{1,0:T(8,128)S(1)}, f32[9,128]{1,0:T(8,128)S(1)}, u32[]{:S(2)}, u32[]{:S(2)}) collective-permute-start(f32[9,128]{1,0:T(8,128)S(1)} %add.164), channel_id=1, source_target_pairs={{0,16},{4,20},{8,24},{12,28},{16,0},{20,4},{24,8},{28,12},{1,17},{... | collective-permute-start | bytes 13832 | tf_op jit(solution)/shard_map/ppermute | solution.py:493
  189.5 1.8 collective-permute-start.32
  (79 other events, 254.3 us)
